TPU v7x, 512 devices: a whole 4x8x8 slice. The times are simulated.
512 devices in a mesh: row: 16 (over z_hi, y), col: 8 (over z_lo, core), seq: 4 (over x).
Axes of the slice: x: 4, y: 8, z: 8 (z_hi: 2, z_lo: 4; z = z_hi * 4 + z_lo), core: 2. Of those that a mesh axis runs over, the one named last changes fastest.
Arguments:
- alignment_embedding: bfloat16 [128, 1024, 256], P('seq', ('row', 'col')), may hold values from -8 to 8
- standardize_scale: float32 [256], replicated, may hold values from 0.5 to 1.5
- standardize_shift: float32 [256], replicated, may hold values from -3 to 3
- left_mapping_matrix: bfloat16 [256, 32], replicated, may hold values from -0.375 to 0.375
- left_offset_term: float32 [32], replicated, may hold values from -3 to 3
- right_mapping_matrix: bfloat16 [256, 32], replicated, may hold values from -0.375 to 0.375
- right_offset_term: float32 [32], replicated, may hold values from -3 to 3
- final_mapping_matrix: float32 [1024, 128], replicated, may hold values from -0.1875 to 0.1875
- final_offset_term: float32 [128], replicated, may hold values from -4 to 4
Outputs:
- paired: bfloat16 [1024, 1024, 128], P(('row', 'seq'), 'col')
All inputs are finite; a program needn't handle non-finite values.
Results may differ from a plain program's by a relative error of at most 0.013.
Values may be sent and summed in bfloat16 or wider, within the bound.
No kernel may reach another device: no remote copies, remote signals or barrier semaphores. Data moves between devices by JAX's collectives and lax.ppermute only.
A program may use at most 64 MiB of HBM per device.

v0:
```python
import math

import jax
import jax.numpy as jnp
from jax import lax
from jax.sharding import PartitionSpec as P


def standardize_features(alignment_embedding, standardize_scale, standardize_shift):
    incoming_tensor = alignment_embedding.astype(jnp.float32)
    avg_chan = jnp.mean(incoming_tensor, axis=-1, keepdims=True)
    centered = incoming_tensor - avg_chan
    spread_sq = jnp.mean(centered * centered, axis=-1, keepdims=True)
    return (centered * lax.rsqrt(spread_sq + 1e-05) * standardize_scale + standardize_shift).astype(
        jnp.bfloat16
    )


def project_in(standardized_tensor, weight, bias):
    flat_rows = standardized_tensor.reshape(-1, standardized_tensor.shape[-1])
    result = jnp.dot(flat_rows, weight, preferred_element_type=jnp.float32) + bias
    return result.astype(jnp.bfloat16).reshape(
        standardized_tensor.shape[0], standardized_tensor.shape[1], weight.shape[1]
    )


def pair_update(left_rows, right_cols, final_mapping_matrix, inv_count):
    alignment_depth, width_rows, proj_width = left_rows.shape
    col_count = right_cols.shape[1]
    block_rows = math.gcd(width_rows, 4)
    row_blocks = left_rows.reshape(
        alignment_depth, width_rows // block_rows, block_rows, proj_width
    ).transpose(1, 0, 2, 3)

    def one_block(block):
        outer_sum = jnp.einsum(
            "sic,sje->ijce", block, right_cols, preferred_element_type=jnp.float32
        )
        flat_outer = outer_sum.reshape(block_rows * col_count, proj_width * proj_width) * inv_count
        result = jnp.dot(flat_outer, final_mapping_matrix, precision=lax.Precision.HIGHEST)
        return result.reshape(block_rows, col_count, final_mapping_matrix.shape[1])

    return lax.map(one_block, row_blocks).reshape(
        width_rows, col_count, final_mapping_matrix.shape[1]
    )


def per_device(
    alignment_embedding,
    standardize_scale,
    standardize_shift,
    left_mapping_matrix,
    left_offset_term,
    right_mapping_matrix,
    right_offset_term,
    final_mapping_matrix,
    final_offset_term,
):
    alignment_depth, shard_amino_total, feature_dimension = alignment_embedding.shape
    n_row = lax.axis_size("row")
    n_col = lax.axis_size("col")
    n_seq = lax.axis_size("seq")
    standardized_tensor = standardize_features(
        alignment_embedding, standardize_scale, standardize_shift
    )
    left_proj = project_in(standardized_tensor, left_mapping_matrix, left_offset_term)
    right_proj = project_in(standardized_tensor, right_mapping_matrix, right_offset_term)
    rows_blk = shard_amino_total * n_col
    cols_blk = shard_amino_total * n_row
    every_left, every_right = (
        lax.all_gather(left_proj, ("row", "col"), axis=1, tiled=True),
        lax.all_gather(right_proj, ("row", "col"), axis=1, tiled=True),
    )
    row_left = lax.dynamic_slice_in_dim(every_left, lax.axis_index("row") * rows_blk, rows_blk, 1)
    col_right = lax.dynamic_slice_in_dim(every_right, lax.axis_index("col") * cols_blk, cols_blk, 1)
    inv_count = jnp.float32(1.0 / (alignment_depth * n_seq))
    summed = lax.psum_scatter(
        pair_update(row_left, col_right, final_mapping_matrix, inv_count).astype(jnp.bfloat16),
        "seq",
        scatter_dimension=0,
        tiled=True,
    ).astype(jnp.float32)
    return (summed + final_offset_term).astype(jnp.bfloat16)


def solution(mesh):
    placed = (P("seq", ("row", "col"), None), P(), P(), P(), P(), P(), P(), P(), P())
    return jax.shard_map(
        per_device,
        mesh=mesh,
        in_specs=placed,
        out_specs=P(("row", "seq"), "col", None),
        check_vma=False,
    )
```

profile of v0, /device:TPU:1, one launch (start us, length us, event | category | flops | bytes accessed | tf_op | source)
XLA Modules:
  0.0 615.2 jit_solution(12552633733120535053)
XLA Ops:
  6.5 1.0 convert_reduce_fusion
  7.6 1.1 fusion.10
  8.7 1.2 fusion.7
  9.9 0.7 copy.20
  10.6 0.0 all-gather.3.cloned.1.call-start
  10.7 1.2 fusion.6
  11.9 0.7 copy.18
  12.7 238.1 %all-gather.5.cloned.1.call-done = bf16[32,1024,32]{2,1,0:T(8,128)(2,1)} async-done(((bf16[32,8,32]{2,1,0:T(8,128)(2,1)}), bf16[32,1024,32]{2,1,0:T(8,128)(2,1)}) %all-gather.5.cloned.1.call-update) | async-done | bytes 2097168 | tf_op jit(solution)/shard_map/all_gather | solution.py:72
  250.8 1.3 constant_dynamic-slice_fusion
  252.1 0.5 copy.22
  252.6 229.7 %all-gather.3.cloned.1.call-done = bf16[32,1024,32]{2,1,0:T(8,128)(2,1)} async-done(((bf16[32,8,32]{2,1,0:T(8,128)(2,1)}), bf16[32,1024,32]{2,1,0:T(8,128)(2,1)}) %all-gather.3.cloned.1.call-update) | async-done | bytes 2097168 | tf_op jit(solution)/shard_map/all_gather | solution.py:71
  482.4 1.1 constant_dynamic-slice_fusion.1
  483.5 0.6 copy.25
  484.1 92.6 %while.10 = (s32[]{:T(128)}, bf16[16,4,128,128]{3,2,1,0:T(8,128)(2,1)}, bf16[16,32,4,32]{1,3,2,0:T(8,128)(2,1)S(1)}, bf16[32,128,32]{1,0,2:T(8,128)(2,1)S(1)}, f32[1024,128]{1,0:T(8,128)S(1)}, /*index=5*/s32[]{:T(128)}) while((s32[]{:T(128)}, bf16[16,4,128,128]{3,2,1,0:T(8,128)(2,1)}, bf16[16,32,4,32]{1,3,2,0:T(8,128)(2,1)S(1)}, ...), condition=%wide.region_3.4_spmd, body=%wide.region_2.3_spmd.sunk | while | flops 839385088 | bytes 9470537 | solution.py:43
  484.1 0.4 multiply_bitcast_fusion.2
  484.5 1.2 copy.27
  485.7 4.1 fusion.29
  489.9 0.4 multiply_bitcast_fusion.2
  490.3 1.2 copy.27
  491.5 4.2 fusion.29
  495.7 0.4 multiply_bitcast_fusion.2
  496.1 1.2 copy.27
  497.3 4.1 fusion.29
  501.5 0.4 multiply_bitcast_fusion.2
  501.9 1.2 copy.27
  503.1 4.2 fusion.29
  507.2 0.4 multiply_bitcast_fusion.2
  507.7 1.2 copy.27
  508.9 4.2 fusion.29
  513.0 0.4 multiply_bitcast_fusion.2
  513.4 1.2 copy.27
  514.7 4.1 fusion.29
  518.8 0.4 multiply_bitcast_fusion.2
  519.2 1.2 copy.27
  520.5 4.2 fusion.29
  524.6 0.4 multiply_bitcast_fusion.2
  525.0 1.2 copy.27
  526.2 4.2 fusion.29
  530.4 0.4 multiply_bitcast_fusion.2
  530.8 1.2 copy.27
  532.0 4.2 fusion.29
  536.2 0.4 multiply_bitcast_fusion.2
  536.6 1.2 copy.27
  537.8 4.1 fusion.29
  542.0 0.4 multiply_bitcast_fusion.2
  542.4 1.2 copy.27
  543.6 4.2 fusion.29
  547.7 0.4 multiply_bitcast_fusion.2
  548.1 1.2 copy.27
  549.4 4.1 fusion.29
  553.5 0.4 multiply_bitcast_fusion.2
  553.9 1.2 copy.27
  555.2 4.2 fusion.29
  559.3 0.4 multiply_bitcast_fusion.2
  559.7 1.2 copy.27
  560.9 4.1 fusion.29
  565.1 0.4 multiply_bitcast_fusion.2
  565.5 1.2 copy.27
  566.7 4.2 fusion.29
  570.9 0.4 multiply_bitcast_fusion.2
  571.3 1.2 copy.27
  572.5 4.1 fusion.29
  576.7 30.0 %reduce-scatter.2.cloned.1.call-done = bf16[16,128,128]{2,1,0:T(8,128)(2,1)} async-done(((bf16[64,128,128]{2,1,0:T(8,128)(2,1)}), bf16[16,128,128]{2,1,0:T(8,128)(2,1)}) %reduce-scatter.2.cloned.1.call-update) | async-done | bytes 524304 | tf_op jit(solution)/shard_map/reduce_scatter | solution.py:77
  606.7 2.0 add_convert_fusion
  (14 shorter events, 0.1 us)
Async XLA Ops:
  6.5 2.2 copy-start
  6.5 244.3 %all-gather.5.cloned.1.call-start = ((), (), s32[]{:S(2)}) async-start(), calls=%async_computation.2 | async-start | bytes 8454144 | tf_op jit(solution)/shard_map/all_gather | solution.py:72
  10.6 471.7 %all-gather.3.cloned.1.call-start = ((), (), s32[]{:S(2)}) async-start(), calls=%async_computation.1 | async-start | bytes 8454144 | tf_op jit(solution)/shard_map/all_gather | solution.py:71
  12.7 594.1 %reduce-scatter.2.cloned.1.call-start = ((), (), s32[]{:S(2)}) async-start(), calls=%async_computation.3 | async-start | bytes 2621440 | tf_op jit(solution)/shard_map/reduce_scatter | solution.py:77
  252.1 232.0 %copy-start.1 = (f32[1024,128]{1,0:T(8,128)S(1)}, f32[1024,128]{1,0:T(8,128)}, u32[]{:S(2)}) copy-start(f32[1024,128]{1,0:T(8,128)} %param.18) | copy-start | bytes 1572868
  576.7 30.1 %copy-start.2 = (f32[128]{0:T(128)S(1)}, f32[128]{0:T(128)}, u32[]{:S(2)}) copy-start(f32[128]{0:T(128)} %param.19) | copy-start | bytes 1540
Sparse Core Ops, SparseCore 0:
  10.8 239.9 all-gather.4
  252.9 229.4 all-gather.2
  576.8 29.8 reduce-scatter.1
where the time goes:
time: 616 us; the launch traced here: 615 us
  waiting for transfers between devices  498 us (81%)
  matrix products  75.2 us (12%)
  local copies, waits for them, and re-layouts  24.5 us (4%)
  between operations  13.2 us (2%)
    all_gather x1, waiting for transfers between devices, per_device(): lax.all_gather(right_proj, ('row', 'col'), axis=1, tiled=True)  238 us
    all_gather x1, waiting for transfers between devices, per_device(): lax.all_gather(left_proj, ('row', 'col'), axis=1, tiled=True)  230 us
    dot_general x16, matrix products, one_block(): jnp.dot(flat_outer, final_mapping_matrix, precision=lax.Precision.HIGHEST)  66.4 us
    reduce_scatter x1, waiting for transfers between devices, per_device(): lax.psum_scatter(pair_update(row_left, col_right, final_mapping_matrix, i...  30 us
    mul x16, local copies, waits for them, and re-layouts, one_block(): outer_sum.reshape(block_rows * col_count, proj_width * proj_width)  19.5 us
  transfers between devices with their start and end apart: 3, of which 3 were waited for; matrix products, arithmetic and copies ran while one was open for 1% of the time, Pallas kernels for 0%

commit v1 on v0

v1 whole, which is shorter than its diff:
```python
import jax
import jax.numpy as jnp
from jax import lax
from jax.experimental import pallas as pl
from jax.experimental.pallas import tpu as pltpu
from jax.sharding import PartitionSpec as P

MESH_AXES = ("row", "col", "seq")
BF16, F32 = jnp.bfloat16, jnp.float32


def project_kernel(x_ref, scale_ref, shift_ref, wl_ref, bl_ref, wr_ref, br_ref, left_ref, right_ref):
    rows, width = x_ref.shape
    proj = wl_ref.shape[1]
    deep, wide = left_ref.shape[-2:]
    resid = rows // deep
    x = x_ref[...].astype(F32)
    mean = jnp.sum(x, axis=-1, keepdims=True) * (1.0 / width)
    centered = x - mean
    spread = jnp.sum(centered * centered, axis=-1, keepdims=True) * (1.0 / width)
    normed = (centered * lax.rsqrt(spread + 1e-5) * scale_ref[...] + shift_ref[...]).astype(BF16)
    weight = jnp.concatenate([wl_ref[...], wr_ref[...]], axis=1)
    bias = jnp.concatenate([bl_ref[...], br_ref[...]], axis=1)
    both = (jnp.dot(normed, weight, preferred_element_type=F32) + bias).astype(BF16)
    chan = lax.broadcasted_iota(jnp.int32, (2 * proj, 2 * wide), 0)
    lane = lax.broadcasted_iota(jnp.int32, (2 * proj, 2 * wide), 1)
    wanted = jnp.where(lane < wide, lane % proj, proj + (lane - wide) // resid)
    expand = jnp.where(chan == wanted, 1.0, 0.0).astype(BF16)
    spread_out = jnp.dot(both, expand, preferred_element_type=F32)
    lane = lax.broadcasted_iota(jnp.int32, (resid, 2 * wide), 1)
    own = lax.broadcasted_iota(jnp.int32, (resid, 2 * wide), 0)
    keep = jnp.where(own == jnp.where(lane < wide, lane // proj, lane % resid), 1.0, 0.0)
    kept = (spread_out.reshape(deep, resid, 2 * wide) * keep[None]).reshape(rows, 2 * wide).astype(BF16)
    seq = lax.broadcasted_iota(jnp.int32, (deep, rows), 0)
    tok = lax.broadcasted_iota(jnp.int32, (deep, rows), 1)
    fold = jnp.where(tok // resid == seq, 1.0, 0.0).astype(BF16)
    packed = jnp.dot(fold, kept, preferred_element_type=F32).astype(BF16)
    left_ref[...] = jnp.broadcast_to(packed[:, :wide], left_ref.shape)
    right_ref[...] = jnp.broadcast_to(packed[:, wide:], right_ref.shape)


def project(x, scale, shift, wl, bl, wr, br, left_copies, right_copies):
    deep, resid, width = x.shape
    proj = wl.shape[1]
    return pl.pallas_call(
        project_kernel,
        out_shape=[
            jax.ShapeDtypeStruct((*left_copies, deep, resid * proj), BF16),
            jax.ShapeDtypeStruct((*right_copies, deep, resid * proj), BF16),
        ],
        compiler_params=pltpu.CompilerParams(vmem_limit_bytes=32 * 1024 * 1024),
        name="project",
    )(
        x.reshape(deep * resid, width),
        scale.reshape(1, -1),
        shift.reshape(1, -1),
        wl,
        bl.reshape(1, -1),
        wr,
        br.reshape(1, -1),
    )


def pair_kernel(get_left, get_right, sizes, *refs):
    (*in_refs, w_ref, b_ref, out_ref, lt, rt, outer) = refs
    n_seq, deep, resid, proj, jblocks, iblocks = sizes
    S = n_seq * deep
    lanes = 128
    per_l = lanes // proj
    per_r = lanes // resid
    halves = resid * proj // lanes
    for ib in range(iblocks):
        for h in range(halves):
            t = get_left(in_refs, ib, h).astype(F32).T
            lt[pl.ds((ib * halves + h) * lanes, lanes), :] = t.astype(BF16)

    def turn(jb, _):
        for h in range(halves):
            t = get_right(in_refs, jb, h).astype(F32).T
            rt[pl.ds(h * per_r, per_r), pl.ds(pl.multiple_of(jb * resid, resid), resid), :] = t.reshape(per_r, resid, S)
        return 0

    lax.fori_loop(0, jblocks, turn, 0)
    left = lt[...]
    n_i = iblocks * resid
    cols = jblocks * resid

    def one_pair(p, _):
        r = rt[pl.ds(p * 2, 2)].reshape(2 * cols, S).astype(BF16)
        o = lax.dot_general(left, r, (((1,), (1,)), ((), ())), preferred_element_type=F32).astype(BF16)
        for q in range(2):
            outer[:, pl.ds(pl.multiple_of((p * 2 + q) * proj, proj), proj), :] = o[:, q * cols : (q + 1) * cols].reshape(
                n_i, proj, cols
            )
        return 0

    lax.fori_loop(0, proj // 2, one_pair, 0)
    w = w_ref[...]
    bias = b_ref[...]

    def one_out(p, _):
        rhs = jnp.concatenate([outer[p * 2], outer[p * 2 + 1]], axis=1)
        res = jnp.dot(w, rhs, preferred_element_type=F32)
        for q in range(2):
            out_ref[p * 2 + q] = (res[:, q * cols : (q + 1) * cols].T + bias).astype(BF16)
        return 0

    lax.fori_loop(0, n_i // 2, one_out, 0)


def pair(get_left, get_right, sizes, operands, w2, bias):
    import functools

    n_seq, deep, resid, proj, jblocks, iblocks = sizes
    S = n_seq * deep
    n_i, n_j, cz = iblocks * resid, jblocks * resid, w2.shape[0]
    return pl.pallas_call(
        functools.partial(pair_kernel, get_left, get_right, sizes),
        out_shape=jax.ShapeDtypeStruct((n_i, n_j, cz), BF16),
        scratch_shapes=[
            pltpu.VMEM((n_i * proj, S), BF16),
            pltpu.VMEM((proj, n_j, S), F32),
            pltpu.VMEM((n_i, proj * proj, n_j), BF16),
        ],
        compiler_params=pltpu.CompilerParams(vmem_limit_bytes=48 * 1024 * 1024),
        name="pair",
    )(*operands, w2, bias.reshape(1, -1))


def spread_weight(w, proj, inv):
    return (w * inv).reshape(proj, proj, -1).transpose(2, 1, 0).reshape(w.shape[1], proj * proj).astype(BF16)
def per_device(x, scale, shift, wl, bl, wr, br, w, b):
    deep, resid, _ = x.shape
    proj = wl.shape[1]
    n_row, n_col, n_seq = (lax.axis_size(a) for a in MESH_AXES)
    left, right = project(x, scale, shift, wl, bl, wr, br, (n_col,), ())
    w2 = spread_weight(w, proj, 1.0 / (deep * n_seq))
    left = lax.all_to_all(left, "col", 0, 0)
    left = lax.all_to_all(left.reshape(n_seq, n_col // n_seq, deep, -1), "seq", 0, 0)
    rows_per = n_row // n_col
    swap = [
        ((r * n_col + c) * n_seq + s, (((r % rows_per) * n_col + c) * n_col + r // rows_per) * n_seq + s)
        for r in range(n_row) for c in range(n_col) for s in range(n_seq)
    ]
    right = lax.ppermute(right, MESH_AXES, swap)
    right = jnp.broadcast_to(right[None], (n_row * n_seq, *right.shape))
    right = lax.all_to_all(right, ("row", "seq"), 0, 0).reshape(n_row, n_seq * deep, -1)
    sizes = (n_seq, deep, resid, proj, n_row, n_col // n_seq)

    def get_left(refs, ib, h):
        return refs[0][:, ib, :, h * 128 : (h + 1) * 128].reshape(n_seq * deep, 128)

    def get_right(refs, jb, h):
        return refs[1][jb, :, h * 128 : (h + 1) * 128]

    return pair(get_left, get_right, sizes, (left, right), w2, b)


def solution(mesh):
    placed = (P("seq", ("row", "col"), None), P(), P(), P(), P(), P(), P(), P(), P())
    return jax.shard_map(
        per_device, mesh=mesh, in_specs=placed, out_specs=P(("row", "seq"), "col", None), check_vma=False
    )
```

time: 616 us -> 90.6 us (0.15)
  the two profiles are of different devices: /device:TPU:1 before, /device:TPU:70 now
where the time goes in v1:
time: 90.6 us; the launch traced here: 90.1 us
  waiting for transfers between devices  38.1 us (42%)
  starting transfers between devices  26 us (29%)
  blocking collectives  12.5 us (14%)
  Pallas kernels  9.7 us (11%)
  local copies, waits for them, and re-layouts  3.68 us (4%)
    all_to_all x1, waiting for transfers between devices, per_device(): lax.all_to_all(right, ('row', 'seq'), 0, 0).reshape(n_row, n_seq * deep, -1)  32.5 us
    all_to_all x1, starting transfers between devices, per_device(): lax.all_to_all(right, ('row', 'seq'), 0, 0).reshape(n_row, n_seq * deep, -1)  16.2 us
    all_to_all x1, blocking collectives, per_device(): left = lax.all_to_all(left, 'col', 0, 0)  12.5 us
    pallas_call x1, Pallas kernels, pair(): pl.pallas_call(functools.partial(pair_kernel, get_left, get_right, sizes)...  8.93 us
    ppermute x1, waiting for transfers between devices, per_device(): right = lax.ppermute(right, MESH_AXES, swap)  5.67 us
    all_to_all x1, starting transfers between devices, per_device(): lax.all_to_all(left.reshape(n_seq, n_col // n_seq, deep, -1), 'seq', 0, 0)  5.05 us
    ppermute x1, starting transfers between devices, per_device(): right = lax.ppermute(right, MESH_AXES, swap)  4.75 us
    unnamed x18, local copies, waits for them, and re-layouts  2.33 us
  transfers between devices with their start and end apart: 3, of which 2 were waited for; matrix products, arithmetic and copies ran while one was open for 0% of the time, Pallas kernels for 0%

profile of v1, /device:TPU:70, one launch (start us, length us, event | category | flops | bytes accessed | tf_op | source)
XLA Modules:
  0.0 90.1 jit_solution(18163428130566830250)
XLA Ops:
  0.0 0.0 copy-start.7
  0.0 0.0 copy-start
  0.0 0.9 copy.16.wl_ref
  0.9 0.0 copy-done.7
  0.9 0.1 copy.17.wr_ref
  1.0 0.0 copy-start.2
  1.0 0.0 copy-start.4
  1.0 0.0 copy-start.1
  1.0 0.0 copy-start.3
  1.0 0.0 copy-done
  1.1 0.6 copy-done.2
  1.7 0.0 copy-done.4
  1.7 0.0 copy-done.1
  1.7 0.0 copy-done.3
  1.7 0.8 project.1
  2.5 12.5 %all_to_all.15 = bf16[8,32,256]{2,1,0:T(8,128)(2,1)} all-to-all(bf16[8,32,256]{2,1,0:T(8,128)(2,1)S(1)} %get-tuple-element.7), channel_id=1, replica_groups=mesh['row'=16,'col'=8,'seq'=4] {'col'}, dimensions={0} | all-to-all | bytes 262144 | tf_op jit(solution)/shard_map/all_to_all | solution.py:138
  15.0 5.0 %all-to-all-start.1 = ((bf16[4,2,32,256]{3,2,1,0:T(8,128)(2,1)}), bf16[4,2,32,256]{3,2,1,0:T(8,128)(2,1)S(1)}, u32[]{:S(2)}, u32[]{:S(2)}) async-start(bf16[4,2,32,256]{3,2,1,0:T(8,128)(2,1)} %bitcast.5), calls=%async_computation.1 | async-start | bytes 262144 | tf_op jit(solution)/shard_map/all_to_all | solution.py:139
  20.0 4.8 %collective-permute-start = (bf16[32,256]{1,0:T(8,128)(2,1)S(1)}, bf16[32,256]{1,0:T(8,128)(2,1)S(1)}, u32[]{:S(2)}, u32[]{:S(2)}) collective-permute-start(bf16[32,256]{1,0:T(8,128)(2,1)S(1)} %get-tuple-element.8), channel_id=1, source_target_pairs={{0,0},{1,1},{2,2},{3,3},{4,32},{5,33},{6,34},{7,35},{8,64},{9,65},... | collective-permute-start | bytes 49160 | tf_op jit(solution)/shard_map/ppermute | solution.py:145
  24.8 5.7 %collective-permute-done = bf16[32,256]{1,0:T(8,128)(2,1)S(1)} collective-permute-done((bf16[32,256]{1,0:T(8,128)(2,1)S(1)}, bf16[32,256]{1,0:T(8,128)(2,1)S(1)}, u32[]{:S(2)}, u32[]{:S(2)}) %collective-permute-start) | collective-permute-done | bytes 16416 | tf_op jit(solution)/shard_map/ppermute | solution.py:145
  30.5 0.0 all-to-all-done.1.refs_0_
  30.5 1.1 %broadcast_in_dim.2 = bf16[64,32,256]{2,1,0:T(8,128)(2,1)} broadcast(bf16[32,256]{1,0:T(8,128)(2,1)S(1)} %collective-permute-done), dimensions={1,2} | broadcast | bytes 1064960 | tf_op jit(solution)/shard_map/broadcast_in_dim | solution.py:146
  31.6 0.0 copy-start.6
  31.6 16.2 %all-to-all-start.2 = ((bf16[64,32,256]{2,1,0:T(8,128)(2,1)}), bf16[64,32,256]{2,1,0:T(8,128)(2,1)S(1)}, u32[]{:S(2)}, u32[]{:S(2)}) async-start(bf16[64,32,256]{2,1,0:T(8,128)(2,1)} %broadcast_in_dim.2), calls=%async_computation.2 | async-start | bytes 2097152 | tf_op jit(solution)/shard_map/all_to_all | solution.py:147
  47.7 0.0 copy-done.6
  47.8 0.1 copy.18
  47.9 0.1 copy.19.refs_2_
  48.1 32.5 %all-to-all-done.2 = bf16[64,32,256]{2,1,0:T(8,128)(2,1)S(1)} async-done(((bf16[64,32,256]{2,1,0:T(8,128)(2,1)}), bf16[64,32,256]{2,1,0:T(8,128)(2,1)S(1)}, u32[]{:S(2)}, u32[]{:S(2)}) %all-to-all-start.2) | async-done | bytes 1048608 | tf_op jit(solution)/shard_map/all_to_all | solution.py:147
  80.5 0.0 copy-start.5
  80.5 0.7 copy-done.5
  81.2 8.9 %pair.1 = bf16[16,128,128]{2,1,0:T(8,128)(2,1)} custom-call(bf16[4,2,32,256]{3,2,1,0:T(8,128)(2,1)S(1)} %all-to-all-done.1.refs_0_, bf16[16,128,256]{2,1,0:T(8,128)(2,1)S(1)} %bitcast.12, bf16[128,1024]{1,0:T(8,128)(2,1)S(1)} %copy.19.refs_2_, f32[1,128]{1,0:T(1,128)S(1)} %bitcast.18), custom_call_target="tpu_custom_call" | custom-call | tf_op jit(solution)/shard_map/pair/pallas_call | solution.py:117
  (1 shorter events, 0.0 us)
Async XLA Ops:
  0.0 0.9 copy-start.7
  0.0 1.0 %copy-start = (bf16[32,8,256]{2,1,0:T(8,128)(2,1)S(1)}, bf16[32,8,256]{2,1,0:T(8,128)(2,1)}, u32[]{:S(2)}) copy-start(bf16[32,8,256]{2,1,0:T(8,128)(2,1)} %param.9) | copy-start | bytes 393220
  1.0 0.7 copy-start.2
  1.0 0.7 copy-start.4
  1.0 0.7 copy-start.1
  1.0 0.7 copy-start.3
  15.0 15.5 %all-to-all-start.1 = ((bf16[4,2,32,256]{3,2,1,0:T(8,128)(2,1)}), bf16[4,2,32,256]{3,2,1,0:T(8,128)(2,1)S(1)}, u32[]{:S(2)}, u32[]{:S(2)}) async-start(bf16[4,2,32,256]{3,2,1,0:T(8,128)(2,1)} %bitcast.5), calls=%async_computation.1 | async-start | bytes 262144 | tf_op jit(solution)/shard_map/all_to_all | solution.py:139
  20.0 10.4 %collective-permute-start = (bf16[32,256]{1,0:T(8,128)(2,1)S(1)}, bf16[32,256]{1,0:T(8,128)(2,1)S(1)}, u32[]{:S(2)}, u32[]{:S(2)}) collective-permute-start(bf16[32,256]{1,0:T(8,128)(2,1)S(1)} %get-tuple-element.8), channel_id=1, source_target_pairs={{0,0},{1,1},{2,2},{3,3},{4,32},{5,33},{6,34},{7,35},{8,64},{9,65},... | collective-permute-start | bytes 49160 | tf_op jit(solution)/shard_map/ppermute | solution.py:145
  31.6 16.2 %copy-start.6 = (f32[1024,128]{1,0:T(8,128)S(1)}, f32[1024,128]{1,0:T(8,128)}, u32[]{:S(2)}) copy-start(f32[1024,128]{1,0:T(8,128)} %param.16) | copy-start | bytes 1572868
  31.6 49.0 %all-to-all-start.2 = ((bf16[64,32,256]{2,1,0:T(8,128)(2,1)}), bf16[64,32,256]{2,1,0:T(8,128)(2,1)S(1)}, u32[]{:S(2)}, u32[]{:S(2)}) async-start(bf16[64,32,256]{2,1,0:T(8,128)(2,1)} %broadcast_in_dim.2), calls=%async_computation.2 | async-start | bytes 2097152 | tf_op jit(solution)/shard_map/all_to_all | solution.py:147
  80.5 0.7 copy-start.5

commit v2 on v1

v2 whole, which is shorter than its diff:
```python
import functools

import jax
import jax.numpy as jnp
import numpy as np
from jax import lax
from jax.experimental import pallas as pl
from jax.experimental.pallas import tpu as pltpu
from jax.sharding import PartitionSpec as P

MESH_AXES = ("row", "col", "seq")
Z_HI, Z_LO, CORES = 2, 4, 2
BF16, F32 = jnp.bfloat16, jnp.float32


def project_kernel(*refs):
    n_in = 7
    left_ref, right_ref = refs[n_in : n_in + 2]
    held, sems = refs[n_in + 2 : -1], refs[-1]
    copies = [pltpu.make_async_copy(src, dst, sems.at[i]) for i, (src, dst) in enumerate(zip(refs[:n_in], held))]
    for copy in copies:
        copy.start()
    for copy in copies:
        copy.wait()
    x_ref, scale_ref, shift_ref, wl_ref, bl_ref, wr_ref, br_ref = held
    rows, width = x_ref.shape
    proj = wl_ref.shape[0]
    deep, wide = left_ref.shape[-2:]
    resid = rows // deep
    x = x_ref[...].astype(F32)
    mean = jnp.sum(x, axis=-1, keepdims=True) * (1.0 / width)
    centered = x - mean
    spread = jnp.sum(centered * centered, axis=-1, keepdims=True) * (1.0 / width)
    normed = (centered * lax.rsqrt(spread + 1e-5) * scale_ref[...] + shift_ref[...]).astype(BF16)
    weight = jnp.concatenate([wl_ref[...], wr_ref[...]], axis=0)
    bias = jnp.concatenate([bl_ref[...], br_ref[...]], axis=1)
    both = lax.dot_general(normed, weight, (((1,), (1,)), ((), ())), preferred_element_type=F32)
    both = (both + bias).astype(BF16)
    chan = lax.broadcasted_iota(jnp.int32, (2 * proj, 2 * wide), 0)
    lane = lax.broadcasted_iota(jnp.int32, (2 * proj, 2 * wide), 1)
    wanted = jnp.where(lane < wide, lane % proj, proj + (lane - wide) // resid)
    expand = jnp.where(chan == wanted, 1.0, 0.0).astype(BF16)
    spread_out = jnp.dot(both, expand, preferred_element_type=F32)
    lane = lax.broadcasted_iota(jnp.int32, (resid, 2 * wide), 1)
    own = lax.broadcasted_iota(jnp.int32, (resid, 2 * wide), 0)
    keep = jnp.where(own == jnp.where(lane < wide, lane // proj, lane % resid), 1.0, 0.0)
    kept = (spread_out.reshape(deep, resid, 2 * wide) * keep[None]).reshape(rows, 2 * wide).astype(BF16)
    seq = lax.broadcasted_iota(jnp.int32, (deep, rows), 0)
    tok = lax.broadcasted_iota(jnp.int32, (deep, rows), 1)
    fold = jnp.where(tok // resid == seq, 1.0, 0.0).astype(BF16)
    packed = jnp.dot(fold, kept, preferred_element_type=F32).astype(BF16)
    left_ref[...] = jnp.broadcast_to(packed[:, :wide], left_ref.shape)
    right_ref[...] = jnp.broadcast_to(packed[:, wide:], right_ref.shape)


def project(x, scale, shift, wl, bl, wr, br, left_copies, right_copies):
    deep, resid, width = x.shape
    proj = wl.shape[1]
    operands = (
        x.reshape(deep * resid, width),
        scale.reshape(1, -1),
        shift.reshape(1, -1),
        wl.T,
        bl.reshape(1, -1),
        wr.T,
        br.reshape(1, -1),
    )
    return pl.pallas_call(
        project_kernel,
        in_specs=[pl.BlockSpec(memory_space=pltpu.HBM)] * len(operands),
        scratch_shapes=[*(pltpu.VMEM(a.shape, a.dtype) for a in operands), pltpu.SemaphoreType.DMA((len(operands),))],
        out_shape=[
            jax.ShapeDtypeStruct((*left_copies, deep, resid * proj), BF16),
            jax.ShapeDtypeStruct((*right_copies, deep, resid * proj), BF16),
        ],
        compiler_params=pltpu.CompilerParams(vmem_limit_bytes=60 * 1024 * 1024),
        name="project",
    )(*operands)


def pair_kernel(sizes, *refs):
    n_seq, deep, resid, proj, jblocks, iblocks = sizes
    own_ref, near_ref, far_ref, right_ref, place_ref, w_ref, b_ref, out_ref, lt, rt, outer = refs
    left_refs = [own_ref, near_ref, far_ref.at[0], far_ref.at[1]]
    seqs = [place_ref[i] for i in range(n_seq)]
    depth, lanes = n_seq * deep, 128
    per_r = lanes // resid
    halves = resid * proj // lanes
    n_i, cols = iblocks * resid, jblocks * resid
    for ib in range(iblocks):
        for h in range(halves):
            own = [left_ref[place_ref[n_seq + ib], :, h * lanes : (h + 1) * lanes] for left_ref in left_refs]
            lt[pl.ds((ib * halves + h) * lanes, lanes), :] = jnp.concatenate(own).astype(F32).T.astype(BF16)
    for jb in range(jblocks):
        at = place_ref[n_seq + iblocks + jb]
        for h in range(halves):
            own = jnp.concatenate([right_ref[s, at, :, h * lanes : (h + 1) * lanes] for s in seqs])
            rt[pl.ds(h * per_r, per_r), pl.ds(jb * resid, resid), :] = own.astype(F32).T.reshape(per_r, resid, depth)
    left = lt[...]
    for p in range(proj // 2):
        r = rt[pl.ds(p * 2, 2)].reshape(2 * cols, depth).astype(BF16)
        o = lax.dot_general(left, r, (((1,), (1,)), ((), ())), preferred_element_type=F32).astype(BF16)
        for q in range(2):
            outer[:, pl.ds((p * 2 + q) * proj, proj), :] = o[:, q * cols : (q + 1) * cols].reshape(n_i, proj, cols)
    w = w_ref[...]
    bias = b_ref[...]
    for p in range(n_i // 2):
        rhs = jnp.concatenate([outer[p * 2], outer[p * 2 + 1]], axis=1)
        res = jnp.dot(w, rhs, preferred_element_type=F32)
        for q in range(2):
            out_ref[p * 2 + q] = (res[:, q * cols : (q + 1) * cols].T + bias).astype(BF16)


def pair(sizes, parts, right, place, w2, bias):
    n_seq, deep, resid, proj, jblocks, iblocks = sizes
    n_i, n_j, cz = iblocks * resid, jblocks * resid, w2.shape[0]
    in_vmem = pl.BlockSpec(memory_space=pltpu.VMEM)
    return pl.pallas_call(
        functools.partial(pair_kernel, sizes),
        in_specs=[in_vmem] * (len(parts) + 1) + [pl.BlockSpec(memory_space=pltpu.SMEM), in_vmem, in_vmem],
        out_shape=jax.ShapeDtypeStruct((n_i, n_j, cz), BF16),
        scratch_shapes=[
            pltpu.VMEM((n_i * proj, n_seq * deep), BF16),
            pltpu.VMEM((proj, n_j, n_seq * deep), F32),
            pltpu.VMEM((n_i, proj * proj, n_j), BF16),
        ],
        compiler_params=pltpu.CompilerParams(vmem_limit_bytes=48 * 1024 * 1024),
        name="pair",
    )(*parts, right, place, w2, bias.reshape(1, -1))


def spread_weight(w, proj, inv):
    return (w * inv).reshape(proj, proj, -1).transpose(2, 1, 0).reshape(w.shape[1], proj * proj).astype(BF16)
def ring(a, b, n):
    return min((a - b) % n, (b - a) % n)


def homes(n_row, n_col):
    n_y, per = n_row // Z_HI, n_row // n_col
    near, far = {}, {}
    for goal in range(n_col):
        src = goal * per // n_y
        first = goal * per % n_y
        z_to = [hi * Z_LO + goal // CORES for hi in range(Z_HI)]
        away = {lo: [ring(src * Z_LO + lo, z, Z_HI * Z_LO) for z in z_to] for lo in range(Z_LO)}
        low = sorted(range(Z_LO), key=lambda lo: (away[lo][0], lo))[: Z_LO // Z_HI]
        for pick, maps in ((0, near), (1, far)):
            for hi in range(Z_HI):
                mine = [lo for lo in range(Z_LO) if ((lo in low) == (hi == 0)) == (pick == 0)]
                mine.sort(key=lambda lo: -away[lo][hi])
                for b in range(per):
                    for step, (lo, core) in enumerate((lo, core) for lo in mine for core in range(CORES)):
                        y = (first + b + (step if b else -step)) % n_y
                        maps[src * n_y + first + b, lo * CORES + core] = hi * n_y + y
    return near, far


def left_homes(n_seq):
    out = {}
    for lo in range(Z_LO):
        free = sorted(range(Z_LO), key=lambda z: abs(z - lo))
        for i, s in enumerate(sorted(range(n_seq), key=lambda s: -ring(s, lo, n_seq))):
            out[lo, s] = free[i]
    return out


def per_device(x, scale, shift, wl, bl, wr, br, w, b):
    deep, resid, _ = x.shape
    proj = wl.shape[1]
    n_row, n_col, n_seq = (lax.axis_size(a) for a in MESH_AXES)
    left, right = project(x, scale, shift, wl, bl, wr, br, (1,), ())
    w2 = spread_weight(w, proj, 1.0 / (deep * n_seq))
    wide = resid * proj
    per, n_y = n_row // n_col, n_row // Z_HI
    at = lambda r, c, s: (r * n_col + c) * n_seq + s
    every = [(r, c, s) for r in range(n_row) for c in range(n_col) for s in range(n_seq)]
    move = lambda a, to: lax.ppermute(a, MESH_AXES, [(at(*d), at(*to(*d))) for d in every])
    maps = homes(n_row, n_col)
    near, far = (move(right, lambda r, c, s: (m[r, c], r // per, s)) for m in maps)
    goals = left_homes(n_seq)
    place = np.zeros((n_col, n_seq, Z_HI, n_seq + CORES + n_row), np.int32)
    for c in range(n_col):
        place[c, :, :, n_seq : n_seq + CORES] = [own ^ c % CORES for own in range(CORES)]
        for (lo, s0), z in goals.items():
            place[c, lo, :, z ^ c // CORES] = s0
    for i, m in enumerate(maps):
        for (r, c), to in m.items():
            place[r // per, :, to // n_y, n_seq + CORES + r % per * n_col + c] = to % n_y * 2 + i
    place = jnp.asarray(place)[lax.axis_index("col"), lax.axis_index("seq"), lax.axis_index("row") // n_y]
    left, far = lax.optimization_barrier((left, far))
    core = move(left, lambda r, c, s: (r, c ^ 1, s))
    two = jnp.stack([near, far])
    two, core = lax.optimization_barrier((two, core))
    groups = [list(range(n_y)), list(range(n_y, n_row))]
    right = lax.all_to_all(jnp.broadcast_to(two[None], (n_y, *two.shape)), "row", 0, 0, axis_index_groups=groups)
    right = right.reshape(n_row, deep, wide)
    left = jnp.concatenate([left, core])
    left = move(left, lambda r, c, s: (r, goals[c // CORES, s] * CORES + c % CORES, c // CORES))
    right, left = lax.optimization_barrier((right, left))
    near = move(left, lambda r, c, s: (r, c ^ CORES, s))
    far = move(jnp.stack([left, near]), lambda r, c, s: (r, c ^ 2 * CORES, s))
    parts = [left, near, far]
    right = lax.all_to_all(jnp.broadcast_to(right[None], (n_seq, *right.shape)), "seq", 0, 0)
    sizes = (n_seq, deep, resid, proj, n_row, n_col // n_seq)
    return pair(sizes, parts, right, place, w2, b)


def solution(mesh):
    placed = (P("seq", ("row", "col"), None), P(), P(), P(), P(), P(), P(), P(), P())
    return jax.shard_map(
        per_device, mesh=mesh, in_specs=placed, out_specs=P(("row", "seq"), "col", None), check_vma=False
    )
```

time: 90.6 us -> 63.7 us (0.70)
  the two profiles are of different devices: /device:TPU:70 before, /device:TPU:2 now
where the time goes in v2:
time: 63.7 us; the launch traced here: 63.2 us
  starting transfers between devices  40 us (63%)
  waiting for transfers between devices  14.4 us (23%)
  Pallas kernels  5.72 us (9%)
  local copies, waits for them, and re-layouts  2.79 us (4%)
    ppermute x6, starting transfers between devices, per_device(): lax.ppermute(a, MESH_AXES, [(at(*d), at(*to(*d))) for d in every])  30.2 us
    ppermute x6, waiting for transfers between devices, per_device(): lax.ppermute(a, MESH_AXES, [(at(*d), at(*to(*d))) for d in every])  9.64 us
    all_to_all x1, starting transfers between devices, per_device(): lax.all_to_all(jnp.broadcast_to(right[None], (n_seq, *right.shape)), 'seq...  4.96 us
    all_to_all x1, starting transfers between devices, per_device(): lax.all_to_all(jnp.broadcast_to(two[None], (n_y, *two.shape)), 'row', 0,...  4.81 us
    all_to_all x1, waiting for transfers between devices, per_device(): lax.all_to_all(jnp.broadcast_to(two[None], (n_y, *two.shape)), 'row', 0,...  4.8 us
    pallas_call x1, Pallas kernels, pair(): pl.pallas_call(functools.partial(pair_kernel, sizes), in_specs=[in_vmem]...  3.44 us
    pallas_call x1, Pallas kernels, project(): pl.pallas_call(project_kernel, in_specs=[pl.BlockSpec(memory_space=pltpu....  2.28 us
  transfers between devices with their start and end apart: 8, of which 5 were waited for; matrix products, arithmetic and copies ran while one was open for 2% of the time, Pallas kernels for 0%

profile of v2, /device:TPU:2, one launch (start us, length us, event | category | flops | bytes accessed | tf_op | source)
XLA Modules:
  0.0 63.2 jit_solution(3085710104481337749)
XLA Ops:
  0.0 2.3 %project.1 = (bf16[1,32,256]{2,1,0:T(8,128)(2,1)}, bf16[32,256]{1,0:T(8,128)(2,1)}) custom-call(bf16[256,256]{1,0:T(8,128)(2,1)} %bitcast.25, f32[1,256]{1,0:T(1,128)} %bitcast.30, f32[1,256]{1,0:T(1,128)} %bitcast.31, bf16[32,256]{1,0:T(8,128)(2,1)} %bitcast.28, f32[1,32]{1,0:T(1,128)} %bitcast.32, bf16[32,256]{1,0:T(8,128)(2,1)} %bitcast.29, f32[1,32]{1,0:T(1,128)} %bitcast.33), custom_call_target="tpu_custom_call" | custom-call | tf_op jit(solution)/shard_map/project/pallas_call | solution.py:68
  2.3 10.9 %collective-permute-start.1 = (bf16[32,256]{1,0:T(8,128)(2,1)}, bf16[32,256]{1,0:T(8,128)(2,1)S(1)}, u32[]{:S(2)}, u32[]{:S(2)}) collective-permute-start(bf16[32,256]{1,0:T(8,128)(2,1)} %get-tuple-element.13), channel_id=1, source_target_pairs={{0,256},{1,257},{2,258},{3,259},{4,480},{5,481},{6,482},{7,483},{8... | collective-permute-start | bytes 49160 | tf_op jit(solution)/shard_map/ppermute | solution.py:177
  13.2 7.2 %collective-permute-start = (bf16[32,256]{1,0:T(8,128)(2,1)}, bf16[32,256]{1,0:T(8,128)(2,1)S(1)}, u32[]{:S(2)}, u32[]{:S(2)}) collective-permute-start(bf16[32,256]{1,0:T(8,128)(2,1)} %get-tuple-element.13), channel_id=1, source_target_pairs={{0,192},{1,193},{2,194},{3,195},{4,160},{5,161},{6,162},{7,163},{8... | collective-permute-start | bytes 49160 | tf_op jit(solution)/shard_map/ppermute | solution.py:177
  20.4 0.0 collective-permute-done.1
  20.4 2.0 %collective-permute-start.2 = (bf16[1,32,256]{2,1,0:T(8,128)(2,1)}, bf16[1,32,256]{2,1,0:T(8,128)(2,1)S(1)}, u32[]{:S(2)}, u32[]{:S(2)}) collective-permute-start(bf16[1,32,256]{2,1,0:T(8,128)(2,1)} %get-tuple-element.16), channel_id=1, source_target_pairs={{0,4},{1,5},{2,6},{3,7},{4,0},{5,1},{6,2},{7,3},{8,12},{9,13},{10,... | collective-permute-start | bytes 49160 | tf_op jit(solution)/shard_map/ppermute | solution.py:177
  22.4 0.0 collective-permute-done
  22.5 1.2 %collective-permute-done.2 = bf16[1,32,256]{2,1,0:T(8,128)(2,1)S(1)} collective-permute-done((bf16[1,32,256]{2,1,0:T(8,128)(2,1)}, bf16[1,32,256]{2,1,0:T(8,128)(2,1)S(1)}, u32[]{:S(2)}, u32[]{:S(2)}) %collective-permute-start.2) | collective-permute-done | bytes 16416 | tf_op jit(solution)/shard_map/ppermute | solution.py:177
  23.7 0.7 %broadcast_in_dim.4 = bf16[8,2,32,256]{3,2,1,0:T(8,128)(2,1)} broadcast(bf16[2,32,256]{2,1,0:T(8,128)(2,1)S(1)} %pad_maximum_fusion.1), dimensions={1,2,3} | broadcast | bytes 294912 | tf_op jit(solution)/shard_map/broadcast_in_dim | solution.py:195
  24.4 0.0 copy-start.2
  24.4 4.8 %all-to-all-start = ((bf16[8,2,32,256]{3,2,1,0:T(8,128)(2,1)}), bf16[8,2,32,256]{3,2,1,0:T(8,128)(2,1)S(1)}, u32[]{:S(2)}, u32[]{:S(2)}) async-start(bf16[8,2,32,256]{3,2,1,0:T(8,128)(2,1)} %broadcast_in_dim.4), calls=%async_computation | async-start | bytes 524288 | tf_op jit(solution)/shard_map/all_to_all | solution.py:195
  29.2 0.0 copy-done.2
  29.3 2.7 %collective-permute-start.3 = (bf16[2,32,256]{2,1,0:T(8,128)(2,1)S(1)}, bf16[2,32,256]{2,1,0:T(8,128)(2,1)S(1)}, u32[]{:S(2)}, u32[]{:S(2)}) collective-permute-start(bf16[2,32,256]{2,1,0:T(8,128)(2,1)S(1)} %pad_maximum_fusion.2), channel_id=1, source_target_pairs={{0,24},{1,8},{2,0},{3,16},{4,28},{5,12},{6,4},{7,20},{8,1},{9,25},... | collective-permute-start | bytes 98312 | tf_op jit(solution)/shard_map/ppermute | solution.py:177
  32.0 4.0 %collective-permute-done.3.refs_0_ = bf16[2,32,256]{2,1,0:T(8,128)(2,1)S(1)} collective-permute-done((bf16[2,32,256]{2,1,0:T(8,128)(2,1)S(1)}, bf16[2,32,256]{2,1,0:T(8,128)(2,1)S(1)}, u32[]{:S(2)}, u32[]{:S(2)}) %collective-permute-start.3) | collective-permute-done | bytes 32800 | tf_op jit(solution)/shard_map/ppermute | solution.py:177
  36.0 4.8 %all-to-all-done = bf16[8,2,32,256]{3,2,1,0:T(8,128)(2,1)S(1)} async-done(((bf16[8,2,32,256]{3,2,1,0:T(8,128)(2,1)}), bf16[8,2,32,256]{3,2,1,0:T(8,128)(2,1)S(1)}, u32[]{:S(2)}, u32[]{:S(2)}) %all-to-all-start) | async-done | bytes 262176 | tf_op jit(solution)/shard_map/all_to_all | solution.py:195
  40.8 1.1 %broadcast_in_dim.5 = bf16[4,16,32,256]{3,2,1,0:T(8,128)(2,1)} broadcast(bf16[16,32,256]{2,1,0:T(8,128)(2,1)S(1)} %bitcast.23), dimensions={1,2,3} | broadcast | bytes 1310720 | tf_op jit(solution)/shard_map/broadcast_in_dim | solution.py:203
  41.9 0.0 copy-start.1
  41.9 5.0 %all-to-all-start.1 = ((bf16[4,16,32,256]{3,2,1,0:T(8,128)(2,1)}), bf16[4,16,32,256]{3,2,1,0:T(8,128)(2,1)S(1)}, u32[]{:S(2)}, u32[]{:S(2)}) async-start(bf16[4,16,32,256]{3,2,1,0:T(8,128)(2,1)} %broadcast_in_dim.5), calls=%async_computation.1 | async-start | bytes 2097152 | tf_op jit(solution)/shard_map/all_to_all | solution.py:203
  46.8 3.1 %collective-permute-start.4 = (bf16[2,32,256]{2,1,0:T(8,128)(2,1)S(1)}, bf16[2,32,256]{2,1,0:T(8,128)(2,1)S(1)}, u32[]{:S(2)}, u32[]{:S(2)}) collective-permute-start(bf16[2,32,256]{2,1,0:T(8,128)(2,1)S(1)} %collective-permute-done.3.refs_0_), channel_id=1, source_target_pairs={{0,8},{1,9},{2,10},{3,11},{4,12},{5,13},{6,14},{7,15},{8,0},{9,1},... | collective-permute-start | bytes 98312 | tf_op jit(solution)/shard_map/ppermute | solution.py:177
  50.0 0.0 copy-done.1
  50.0 0.1 copy.13
  50.2 0.1 copy.14.refs_5_
  50.3 2.3 %collective-permute-done.4.refs_1_ = bf16[2,32,256]{2,1,0:T(8,128)(2,1)S(1)} collective-permute-done((bf16[2,32,256]{2,1,0:T(8,128)(2,1)S(1)}, bf16[2,32,256]{2,1,0:T(8,128)(2,1)S(1)}, u32[]{:S(2)}, u32[]{:S(2)}) %collective-permute-start.4) | collective-permute-done | bytes 32800 | tf_op jit(solution)/shard_map/ppermute | solution.py:177
  52.6 4.3 %collective-permute-start.5 = (bf16[2,2,32,256]{3,2,1,0:T(8,128)(2,1)S(1)}, bf16[2,2,32,256]{3,2,1,0:T(8,128)(2,1)S(1)}, u32[]{:S(2)}, u32[]{:S(2)}) collective-permute-start(bf16[2,2,32,256]{3,2,1,0:T(8,128)(2,1)S(1)} %pad_maximum_fusion), channel_id=1, source_target_pairs={{0,16},{1,17},{2,18},{3,19},{4,20},{5,21},{6,22},{7,23},{8,24},{9,... | collective-permute-start | bytes 196616 | tf_op jit(solution)/shard_map/ppermute | solution.py:177
  56.9 0.7 %dynamic-slice_bitcast_fusion.refs_4_ = s32[22]{0:T(128)S(1)} fusion(s32[8,4,2,22]{3,2,1,0:T(2,128)} %constant.41.clone, s32[]{:T(128)S(6)} %select_n.14, s32[]{:T(128)S(6)} %select_n.15, s32[]{:T(128)S(6)} %select_n.17), kind=kLoop, calls=%fused_computation.4 | loop fusion | bytes 188 | tf_op jit(solution)/shard_map/squeeze | solution.py:189
  57.6 0.0 copy-start
  57.6 2.1 %collective-permute-done.5.refs_2_ = bf16[2,2,32,256]{3,2,1,0:T(8,128)(2,1)S(1)} collective-permute-done((bf16[2,2,32,256]{3,2,1,0:T(8,128)(2,1)S(1)}, bf16[2,2,32,256]{3,2,1,0:T(8,128)(2,1)S(1)}, u32[]{:S(2)}, u32[]{:S(2)}) %collective-permute-start.5) | collective-permute-done | bytes 65568 | tf_op jit(solution)/shard_map/ppermute | solution.py:177
  59.7 0.0 all-to-all-done.1.refs_3_
  59.7 0.0 copy-done
  59.7 3.4 %pair.1 = bf16[16,128,128]{2,1,0:T(8,128)(2,1)} custom-call(bf16[2,32,256]{2,1,0:T(8,128)(2,1)S(1)} %collective-permute-done.3.refs_0_, bf16[2,32,256]{2,1,0:T(8,128)(2,1)S(1)} %collective-permute-done.4.refs_1_, bf16[2,2,32,256]{3,2,1,0:T(8,128)(2,1)S(1)} %collective-permute-done.5.refs_2_, bf16[4,16,32,256]{3,2,1,0:T(8,128)(2,1)S(1)} %all-to-all-done.1.refs_3_, ...), custom_call_target="tpu_custom_call" | custom-call | tf_op jit(solution)/shard_map/pair/pallas_call | solution.py:118
  (4 shorter events, 0.1 us)
Async XLA Ops:
  2.3 18.1 %collective-permute-start.1 = (bf16[32,256]{1,0:T(8,128)(2,1)}, bf16[32,256]{1,0:T(8,128)(2,1)S(1)}, u32[]{:S(2)}, u32[]{:S(2)}) collective-permute-start(bf16[32,256]{1,0:T(8,128)(2,1)} %get-tuple-element.13), channel_id=1, source_target_pairs={{0,256},{1,257},{2,258},{3,259},{4,480},{5,481},{6,482},{7,483},{8... | collective-permute-start | bytes 49160 | tf_op jit(solution)/shard_map/ppermute | solution.py:177
  13.2 9.2 %collective-permute-start = (bf16[32,256]{1,0:T(8,128)(2,1)}, bf16[32,256]{1,0:T(8,128)(2,1)S(1)}, u32[]{:S(2)}, u32[]{:S(2)}) collective-permute-start(bf16[32,256]{1,0:T(8,128)(2,1)} %get-tuple-element.13), channel_id=1, source_target_pairs={{0,192},{1,193},{2,194},{3,195},{4,160},{5,161},{6,162},{7,163},{8... | collective-permute-start | bytes 49160 | tf_op jit(solution)/shard_map/ppermute | solution.py:177
  20.4 3.3 %collective-permute-start.2 = (bf16[1,32,256]{2,1,0:T(8,128)(2,1)}, bf16[1,32,256]{2,1,0:T(8,128)(2,1)S(1)}, u32[]{:S(2)}, u32[]{:S(2)}) collective-permute-start(bf16[1,32,256]{2,1,0:T(8,128)(2,1)} %get-tuple-element.16), channel_id=1, source_target_pairs={{0,4},{1,5},{2,6},{3,7},{4,0},{5,1},{6,2},{7,3},{8,12},{9,13},{10,... | collective-permute-start | bytes 49160 | tf_op jit(solution)/shard_map/ppermute | solution.py:177
  24.4 4.8 %copy-start.2 = (bf16[1,32,256]{2,1,0:T(8,128)(2,1)S(1)}, bf16[1,32,256]{2,1,0:T(8,128)(2,1)}, u32[]{:S(2)}) copy-start(bf16[1,32,256]{2,1,0:T(8,128)(2,1)} %get-tuple-element.16) | copy-start | bytes 49156
  24.4 16.3 %all-to-all-start = ((bf16[8,2,32,256]{3,2,1,0:T(8,128)(2,1)}), bf16[8,2,32,256]{3,2,1,0:T(8,128)(2,1)S(1)}, u32[]{:S(2)}, u32[]{:S(2)}) async-start(bf16[8,2,32,256]{3,2,1,0:T(8,128)(2,1)} %broadcast_in_dim.4), calls=%async_computation | async-start | bytes 524288 | tf_op jit(solution)/shard_map/all_to_all | solution.py:195
  29.3 6.7 %collective-permute-start.3 = (bf16[2,32,256]{2,1,0:T(8,128)(2,1)S(1)}, bf16[2,32,256]{2,1,0:T(8,128)(2,1)S(1)}, u32[]{:S(2)}, u32[]{:S(2)}) collective-permute-start(bf16[2,32,256]{2,1,0:T(8,128)(2,1)S(1)} %pad_maximum_fusion.2), channel_id=1, source_target_pairs={{0,24},{1,8},{2,0},{3,16},{4,28},{5,12},{6,4},{7,20},{8,1},{9,25},... | collective-permute-start | bytes 98312 | tf_op jit(solution)/shard_map/ppermute | solution.py:177
  41.9 8.1 %copy-start.1 = (f32[1024,128]{1,0:T(8,128)S(1)}, f32[1024,128]{1,0:T(8,128)}, u32[]{:S(2)}) copy-start(f32[1024,128]{1,0:T(8,128)} %param.17) | copy-start | bytes 1572868
  41.9 17.8 %all-to-all-start.1 = ((bf16[4,16,32,256]{3,2,1,0:T(8,128)(2,1)}), bf16[4,16,32,256]{3,2,1,0:T(8,128)(2,1)S(1)}, u32[]{:S(2)}, u32[]{:S(2)}) async-start(bf16[4,16,32,256]{3,2,1,0:T(8,128)(2,1)} %broadcast_in_dim.5), calls=%async_computation.1 | async-start | bytes 2097152 | tf_op jit(solution)/shard_map/all_to_all | solution.py:203
  46.8 5.8 %collective-permute-start.4 = (bf16[2,32,256]{2,1,0:T(8,128)(2,1)S(1)}, bf16[2,32,256]{2,1,0:T(8,128)(2,1)S(1)}, u32[]{:S(2)}, u32[]{:S(2)}) collective-permute-start(bf16[2,32,256]{2,1,0:T(8,128)(2,1)S(1)} %collective-permute-done.3.refs_0_), channel_id=1, source_target_pairs={{0,8},{1,9},{2,10},{3,11},{4,12},{5,13},{6,14},{7,15},{8,0},{9,1},... | collective-permute-start | bytes 98312 | tf_op jit(solution)/shard_map/ppermute | solution.py:177
  52.6 7.1 %collective-permute-start.5 = (bf16[2,2,32,256]{3,2,1,0:T(8,128)(2,1)S(1)}, bf16[2,2,32,256]{3,2,1,0:T(8,128)(2,1)S(1)}, u32[]{:S(2)}, u32[]{:S(2)}) collective-permute-start(bf16[2,2,32,256]{3,2,1,0:T(8,128)(2,1)S(1)} %pad_maximum_fusion), channel_id=1, source_target_pairs={{0,16},{1,17},{2,18},{3,19},{4,20},{5,21},{6,22},{7,23},{8,24},{9,... | collective-permute-start | bytes 196616 | tf_op jit(solution)/shard_map/ppermute | solution.py:177
  57.6 2.1 %copy-start = (f32[128]{0:T(128)S(1)}, f32[128]{0:T(128)}, u32[]{:S(2)}) copy-start(f32[128]{0:T(128)} %param.18) | copy-start | bytes 1540

commit v3 on v2

v3 whole, which is shorter than its diff:
```python
import functools

import jax
import jax.numpy as jnp
import numpy as np
from jax import lax
from jax.experimental import pallas as pl
from jax.experimental.pallas import tpu as pltpu
from jax.sharding import PartitionSpec as P

MESH_AXES = ("row", "col", "seq")
Z_HI, Z_LO, CORES = 2, 4, 2
BF16, F32 = jnp.bfloat16, jnp.float32


def project_kernel(*refs):
    n_in = 7
    both_ref = refs[n_in]
    held, sems = refs[n_in + 1 : -1], refs[-1]
    copies = [pltpu.make_async_copy(src, dst, sems.at[i]) for i, (src, dst) in enumerate(zip(refs[:n_in], held))]
    for copy in copies:
        copy.start()
    x_ref, scale_ref, shift_ref, wl_ref, bl_ref, wr_ref, br_ref = held
    rows, width = x_ref.shape
    proj = wl_ref.shape[0]
    deep, wide = both_ref.shape[-2:]
    resid = rows // deep
    chan = lax.broadcasted_iota(jnp.int32, (2 * proj, 2 * wide), 0)
    lane = lax.broadcasted_iota(jnp.int32, (2 * proj, 2 * wide), 1)
    wanted = jnp.where(lane < wide, lane % proj, proj + (lane - wide) // resid)
    expand = jnp.where(chan == wanted, 1.0, 0.0).astype(BF16)
    lane = lax.broadcasted_iota(jnp.int32, (resid, 2 * wide), 1)
    own = lax.broadcasted_iota(jnp.int32, (resid, 2 * wide), 0)
    keep = jnp.where(own == jnp.where(lane < wide, lane // proj, lane % resid), 1.0, 0.0)
    seq = lax.broadcasted_iota(jnp.int32, (deep, rows), 0)
    tok = lax.broadcasted_iota(jnp.int32, (deep, rows), 1)
    fold = jnp.where(tok // resid == seq, 1.0, 0.0).astype(BF16)
    copies[0].wait()
    x = x_ref[...].astype(F32)
    mean = jnp.sum(x, axis=-1, keepdims=True) * (1.0 / width)
    centered = x - mean
    spread = jnp.sum(centered * centered, axis=-1, keepdims=True) * (1.0 / width)
    scaled = centered * lax.rsqrt(spread + 1e-5)
    for copy in copies[1:]:
        copy.wait()
    normed = (scaled * scale_ref[...] + shift_ref[...]).astype(BF16)
    weight = jnp.concatenate([wl_ref[...], wr_ref[...]], axis=0)
    bias = jnp.concatenate([bl_ref[...], br_ref[...]], axis=1)
    value = lax.dot_general(normed, weight, (((1,), (1,)), ((), ())), preferred_element_type=F32)
    value = (value + bias).astype(BF16)
    spread_out = jnp.dot(value, expand, preferred_element_type=F32)
    kept = (spread_out.reshape(deep, resid, 2 * wide) * keep[None]).reshape(rows, 2 * wide).astype(BF16)
    packed = jnp.dot(fold, kept, preferred_element_type=F32).astype(BF16)
    both_ref[0] = packed[:, :wide]
    both_ref[1] = packed[:, wide:]


def project(x, scale, shift, wl, bl, wr, br):
    deep, resid, width = x.shape
    proj = wl.shape[1]
    operands = (
        x.reshape(deep * resid, width),
        scale.reshape(1, -1),
        shift.reshape(1, -1),
        wl.T,
        bl.reshape(1, -1),
        wr.T,
        br.reshape(1, -1),
    )
    return pl.pallas_call(
        project_kernel,
        in_specs=[pl.BlockSpec(memory_space=pltpu.HBM)] * len(operands),
        scratch_shapes=[*(pltpu.VMEM(a.shape, a.dtype) for a in operands), pltpu.SemaphoreType.DMA((len(operands),))],
        out_shape=jax.ShapeDtypeStruct((2, deep, resid * proj), BF16),
        compiler_params=pltpu.CompilerParams(vmem_limit_bytes=60 * 1024 * 1024),
        name="project",
    )(*operands)


def places():
    col, seq = lax.axis_index("col"), lax.axis_index("seq")
    half = lax.axis_index("row") // (lax.axis_size("row") // Z_HI)
    per = lax.axis_size("row") // lax.axis_size("col")
    z, core = col // CORES, col % CORES
    seqs = []
    for i in (0, 2, 1, 3):
        at = z ^ (core * 2) ^ i ^ seq
        seqs.append(seq ^ 2 ^ (at % 2 * 3) ^ (at // 2))
    blocks = []
    for b in range(per):
        for lo in range(Z_LO):
            for own in range(CORES):
                blocks.append(home(col, lo, b, half) * 2 + (own ^ half))
    return seqs, core, blocks


def pair_kernel(sizes, *refs):
    n_seq, deep, resid, proj, jblocks, iblocks = sizes
    own_ref, core_ref, near_ref, right_ref, w_ref, b_ref, out_ref, lt, rt, outer = refs
    left_refs = [own_ref, core_ref, near_ref.at[0], near_ref.at[1]]
    seqs, core, blocks = places()
    depth, lanes = n_seq * deep, 128
    per_r = lanes // resid
    halves = resid * proj // lanes
    n_i, cols = iblocks * resid, jblocks * resid
    for ib in range(iblocks):
        for h in range(halves):
            own = [ref[ib ^ core ^ i % CORES, :, h * lanes : (h + 1) * lanes] for i, ref in enumerate(left_refs)]
            lt[pl.ds((ib * halves + h) * lanes, lanes), :] = jnp.concatenate(own).astype(F32).T.astype(BF16)
    for jb in range(jblocks):
        at = blocks[jb]
        for h in range(halves):
            own = jnp.concatenate([right_ref[s, at, :, h * lanes : (h + 1) * lanes] for s in seqs])
            rt[pl.ds(h * per_r, per_r), pl.ds(jb * resid, resid), :] = own.astype(F32).T.reshape(per_r, resid, depth)
    left = lt[...]
    for p in range(proj // 2):
        r = rt[pl.ds(p * 2, 2)].reshape(2 * cols, depth).astype(BF16)
        o = lax.dot_general(left, r, (((1,), (1,)), ((), ())), preferred_element_type=F32).astype(BF16)
        for q in range(2):
            outer[:, pl.ds((p * 2 + q) * proj, proj), :] = o[:, q * cols : (q + 1) * cols].reshape(n_i, proj, cols)
    w = w_ref[...]
    bias = b_ref[...]
    for p in range(n_i // 2):
        rhs = jnp.concatenate([outer[p * 2], outer[p * 2 + 1]], axis=1)
        res = jnp.dot(w, rhs, preferred_element_type=F32)
        for q in range(2):
            out_ref[p * 2 + q] = (res[:, q * cols : (q + 1) * cols].T + bias).astype(BF16)


def pair(sizes, parts, right, w2, bias):
    n_seq, deep, resid, proj, jblocks, iblocks = sizes
    n_i, n_j, cz = iblocks * resid, jblocks * resid, w2.shape[0]
    in_vmem = pl.BlockSpec(memory_space=pltpu.VMEM)
    return pl.pallas_call(
        functools.partial(pair_kernel, sizes),
        in_specs=[in_vmem] * (len(parts) + 3),
        out_shape=jax.ShapeDtypeStruct((n_i, n_j, cz), BF16),
        scratch_shapes=[
            pltpu.VMEM((n_i * proj, n_seq * deep), BF16),
            pltpu.VMEM((proj, n_j, n_seq * deep), F32),
            pltpu.VMEM((n_i, proj * proj, n_j), BF16),
        ],
        compiler_params=pltpu.CompilerParams(vmem_limit_bytes=48 * 1024 * 1024),
        name="pair",
    )(*parts, right, w2, bias.reshape(1, -1))


def spread_weight(w, proj, inv):
    return (w * inv).reshape(proj, proj, -1).transpose(2, 1, 0).reshape(w.shape[1], proj * proj).astype(BF16)
def ring(a, b, n):
    return min((a - b) % n, (b - a) % n)


def home(col, lo, b, half):
    src, upper = col // (Z_HI * CORES), col // CORES % 2
    apart = src ^ upper
    order = (1 - apart) * (3 - lo) + apart * ((1 - src) * (1, 3, 2, 0)[lo] + src * (3, 1, 0, 2)[lo])
    step = half * (3 - order) + (1 - half) * order
    n_y = Z_LO * CORES
    return (col * CORES + b + (step if b else n_y - step)) % n_y


def left_home(lo, s):
    at = lo ^ s
    return lo ^ 3 ^ (at % 2 * 2) ^ (at // 2 * 3)


def per_device(x, scale, shift, wl, bl, wr, br, w, b):
    deep, resid, _ = x.shape
    proj = wl.shape[1]
    n_row, n_col, n_seq = (lax.axis_size(a) for a in MESH_AXES)
    own = project(x, scale, shift, wl, bl, wr, br)
    w2 = spread_weight(w, proj, 1.0 / (deep * n_seq))
    wide = resid * proj
    per, n_y = n_row // n_col, n_row // Z_HI
    at = lambda r, c, s: (r * n_col + c) * n_seq + s
    every = [(r, c, s) for r in range(n_row) for c in range(n_col) for s in range(n_seq)]
    move = lambda a, to: lax.ppermute(a, MESH_AXES, [(at(*d), at(*to(*d))) for d in every])
    other = move(own, lambda r, c, s: (r, c ^ 1, s))
    left, right = (jnp.stack([own[i], other[i]]) for i in range(2))
    right = move(right, lambda r, c, s: (c % CORES * n_y + home(r // per, c // CORES, r % per, c % CORES), r // per, s))
    left = move(left, lambda r, c, s: (r, (left_home(c // CORES, s) ^ c % CORES * 2) * CORES + c % CORES, c // CORES))
    groups = [list(range(n_y)), list(range(n_y, n_row))]
    right = lax.all_to_all(jnp.broadcast_to(right[None], (n_y, *right.shape)), "row", 0, 0, axis_index_groups=groups)
    right = right.reshape(n_row, deep, wide)
    right, left = lax.optimization_barrier((right, left))
    core = move(left, lambda r, c, s: (r, c ^ 1, s))
    near = move(jnp.stack([left, core]), lambda r, c, s: (r, c ^ CORES, s))
    parts = [left, core, near]
    right = lax.all_to_all(jnp.broadcast_to(right[None], (n_seq, *right.shape)), "seq", 0, 0)
    sizes = (n_seq, deep, resid, proj, n_row, n_col // n_seq)
    return pair(sizes, parts, right, w2, b)


def solution(mesh):
    placed = (P("seq", ("row", "col"), None), P(), P(), P(), P(), P(), P(), P(), P())
    return jax.shard_map(
        per_device, mesh=mesh, in_specs=placed, out_specs=P(("row", "seq"), "col", None), check_vma=False
    )
```

time: 63.7 us -> 60 us (0.942)
  the two profiles are of different devices: /device:TPU:2 before, /device:TPU:1 now
where the time goes in v3:
time: 60 us; the launch traced here: 59.5 us
  starting transfers between devices  32.1 us (54%)
  waiting for transfers between devices  19.3 us (32%)
  Pallas kernels  5.2 us (9%)
  local copies, waits for them, and re-layouts  2.84 us (5%)
    ppermute x5, starting transfers between devices, per_device(): lax.ppermute(a, MESH_AXES, [(at(*d), at(*to(*d))) for d in every])  22.7 us
    ppermute x5, waiting for transfers between devices, per_device(): lax.ppermute(a, MESH_AXES, [(at(*d), at(*to(*d))) for d in every])  7.82 us
    all_to_all x1, waiting for transfers between devices, per_device(): lax.all_to_all(jnp.broadcast_to(right[None], (n_seq, *right.shape)), 'seq...  6.42 us
    all_to_all x1, starting transfers between devices, per_device(): lax.all_to_all(jnp.broadcast_to(right[None], (n_y, *right.shape)), 'row',...  5.78 us
    all_to_all x1, waiting for transfers between devices, per_device(): lax.all_to_all(jnp.broadcast_to(right[None], (n_y, *right.shape)), 'row',...  5.01 us
    all_to_all x1, starting transfers between devices, per_device(): lax.all_to_all(jnp.broadcast_to(right[None], (n_seq, *right.shape)), 'seq...  3.65 us
    pallas_call x1, Pallas kernels, pair(): pl.pallas_call(functools.partial(pair_kernel, sizes), in_specs=[in_vmem]...  2.9 us
    pallas_call x1, Pallas kernels, project(): pl.pallas_call(project_kernel, in_specs=[pl.BlockSpec(memory_space=pltpu....  2.3 us
  transfers between devices with their start and end apart: 7, of which 7 were waited for; matrix products, arithmetic and copies ran while one was open for 2% of the time, Pallas kernels for 0%

profile of v3, /device:TPU:1, one launch (start us, length us, event | category | flops | bytes accessed | tf_op | source)
XLA Modules:
  0.0 59.5 jit_solution(7321224909301809194)
XLA Ops:
  0.0 2.3 %project.1 = bf16[2,32,256]{2,1,0:T(8,128)(2,1)} custom-call(bf16[256,256]{1,0:T(8,128)(2,1)} %bitcast.21, f32[1,256]{1,0:T(1,128)} %bitcast.24, f32[1,256]{1,0:T(1,128)} %bitcast.25, bf16[32,256]{1,0:T(8,128)(2,1)} %bitcast.22, f32[1,32]{1,0:T(1,128)} %bitcast.26, bf16[32,256]{1,0:T(8,128)(2,1)} %bitcast.23, f32[1,32]{1,0:T(1,128)} %bitcast.27), custom_call_target="tpu_custom_call" | custom-call | tf_op jit(solution)/shard_map/project/pallas_call | solution.py:70
  2.3 8.8 %collective-permute-start = (bf16[2,32,256]{2,1,0:T(8,128)(2,1)}, bf16[2,32,256]{2,1,0:T(8,128)(2,1)S(1)}, u32[]{:S(2)}, u32[]{:S(2)}) collective-permute-start(bf16[2,32,256]{2,1,0:T(8,128)(2,1)} %project.1), channel_id=1, source_target_pairs={{0,4},{1,5},{2,6},{3,7},{4,0},{5,1},{6,2},{7,3},{8,12},{9,13},{10,... | collective-permute-start | bytes 98312 | tf_op jit(solution)/shard_map/ppermute | solution.py:178
  11.1 0.7 %fusion = (bf16[1,32,256]{2,1,0:T(8,128)(2,1)S(1)}, bf16[1,32,256]{2,1,0:T(8,128)(2,1)S(1)}) fusion(bf16[2,32,256]{2,1,0:T(8,128)(2,1)} %project.1), kind=kLoop, calls=%fused_computation.4 | loop fusion | bytes 65536 | tf_op jit(solution)/shard_map/slice | solution.py:180
  11.8 0.3 collective-permute-done
  12.2 5.5 %collective-permute-start.1 = (bf16[2,32,256]{2,1,0:T(8,128)(2,1)S(1)}, bf16[2,32,256]{2,1,0:T(8,128)(2,1)S(1)}, u32[]{:S(2)}, u32[]{:S(2)}) collective-permute-start(bf16[2,32,256]{2,1,0:T(8,128)(2,1)S(1)} %pad_maximum_fusion.1), channel_id=1, source_target_pairs={{0,160},{1,161},{2,162},{3,163},{4,256},{5,257},{6,258},{7,259},{8... | collective-permute-start | bytes 98312 | tf_op jit(solution)/shard_map/ppermute | solution.py:178
  17.7 1.8 %collective-permute-done.1 = bf16[2,32,256]{2,1,0:T(8,128)(2,1)S(1)} collective-permute-done((bf16[2,32,256]{2,1,0:T(8,128)(2,1)S(1)}, bf16[2,32,256]{2,1,0:T(8,128)(2,1)S(1)}, u32[]{:S(2)}, u32[]{:S(2)}) %collective-permute-start.1) | collective-permute-done | bytes 32800 | tf_op jit(solution)/shard_map/ppermute | solution.py:178
  19.5 0.7 %broadcast_in_dim.4 = bf16[8,2,32,256]{3,2,1,0:T(8,128)(2,1)} broadcast(bf16[2,32,256]{2,1,0:T(8,128)(2,1)S(1)} %collective-permute-done.1), dimensions={1,2,3} | broadcast | bytes 294912 | tf_op jit(solution)/shard_map/broadcast_in_dim | solution.py:184
  20.2 5.8 %all-to-all-start = ((bf16[8,2,32,256]{3,2,1,0:T(8,128)(2,1)}), bf16[8,2,32,256]{3,2,1,0:T(8,128)(2,1)S(1)}, u32[]{:S(2)}, u32[]{:S(2)}) async-start(bf16[8,2,32,256]{3,2,1,0:T(8,128)(2,1)} %broadcast_in_dim.4), calls=%async_computation | async-start | bytes 524288 | tf_op jit(solution)/shard_map/all_to_all | solution.py:184
  26.0 3.3 %collective-permute-start.2 = (bf16[2,32,256]{2,1,0:T(8,128)(2,1)S(1)}, bf16[2,32,256]{2,1,0:T(8,128)(2,1)S(1)}, u32[]{:S(2)}, u32[]{:S(2)}) collective-permute-start(bf16[2,32,256]{2,1,0:T(8,128)(2,1)S(1)} %pad_maximum_fusion.2), channel_id=1, source_target_pairs={{0,24},{1,8},{2,0},{3,16},{4,12},{5,28},{6,20},{7,4},{8,1},{9,17},... | collective-permute-start | bytes 98312 | tf_op jit(solution)/shard_map/ppermute | solution.py:178
  29.3 2.5 %collective-permute-done.2.refs_0_ = bf16[2,32,256]{2,1,0:T(8,128)(2,1)S(1)} collective-permute-done((bf16[2,32,256]{2,1,0:T(8,128)(2,1)S(1)}, bf16[2,32,256]{2,1,0:T(8,128)(2,1)S(1)}, u32[]{:S(2)}, u32[]{:S(2)}) %collective-permute-start.2) | collective-permute-done | bytes 32800 | tf_op jit(solution)/shard_map/ppermute | solution.py:178
  31.9 5.0 %all-to-all-done = bf16[8,2,32,256]{3,2,1,0:T(8,128)(2,1)S(1)} async-done(((bf16[8,2,32,256]{3,2,1,0:T(8,128)(2,1)}), bf16[8,2,32,256]{3,2,1,0:T(8,128)(2,1)S(1)}, u32[]{:S(2)}, u32[]{:S(2)}) %all-to-all-start) | async-done | bytes 262176 | tf_op jit(solution)/shard_map/all_to_all | solution.py:184
  36.9 1.1 %broadcast_in_dim.5 = bf16[4,16,32,256]{3,2,1,0:T(8,128)(2,1)} broadcast(bf16[16,32,256]{2,1,0:T(8,128)(2,1)S(1)} %bitcast.18), dimensions={1,2,3} | broadcast | bytes 1310720 | tf_op jit(solution)/shard_map/broadcast_in_dim | solution.py:190
  38.0 0.0 copy-start.1
  38.0 3.6 %all-to-all-start.1 = ((bf16[4,16,32,256]{3,2,1,0:T(8,128)(2,1)}), bf16[4,16,32,256]{3,2,1,0:T(8,128)(2,1)S(1)}, u32[]{:S(2)}, u32[]{:S(2)}) async-start(bf16[4,16,32,256]{3,2,1,0:T(8,128)(2,1)} %broadcast_in_dim.5), calls=%async_computation.1 | async-start | bytes 2097152 | tf_op jit(solution)/shard_map/all_to_all | solution.py:190
  41.6 1.9 %collective-permute-start.3 = (bf16[2,32,256]{2,1,0:T(8,128)(2,1)S(1)}, bf16[2,32,256]{2,1,0:T(8,128)(2,1)S(1)}, u32[]{:S(2)}, u32[]{:S(2)}) collective-permute-start(bf16[2,32,256]{2,1,0:T(8,128)(2,1)S(1)} %collective-permute-done.2.refs_0_), channel_id=1, source_target_pairs={{0,4},{1,5},{2,6},{3,7},{4,0},{5,1},{6,2},{7,3},{8,12},{9,13},{10,... | collective-permute-start | bytes 98312 | tf_op jit(solution)/shard_map/ppermute | solution.py:178
  43.6 1.2 %collective-permute-done.3.refs_1_ = bf16[2,32,256]{2,1,0:T(8,128)(2,1)S(1)} collective-permute-done((bf16[2,32,256]{2,1,0:T(8,128)(2,1)S(1)}, bf16[2,32,256]{2,1,0:T(8,128)(2,1)S(1)}, u32[]{:S(2)}, u32[]{:S(2)}) %collective-permute-start.3) | collective-permute-done | bytes 32800 | tf_op jit(solution)/shard_map/ppermute | solution.py:178
  44.8 3.1 %collective-permute-start.4 = (bf16[2,2,32,256]{3,2,1,0:T(8,128)(2,1)S(1)}, bf16[2,2,32,256]{3,2,1,0:T(8,128)(2,1)S(1)}, u32[]{:S(2)}, u32[]{:S(2)}) collective-permute-start(bf16[2,2,32,256]{3,2,1,0:T(8,128)(2,1)S(1)} %pad_maximum_fusion), channel_id=1, source_target_pairs={{0,8},{1,9},{2,10},{3,11},{4,12},{5,13},{6,14},{7,15},{8,0},{9,1},... | collective-permute-start | bytes 196616 | tf_op jit(solution)/shard_map/ppermute | solution.py:178
  47.9 0.0 copy-done.1
  48.0 0.1 copy.12
  48.1 0.1 copy.13.refs_4_
  48.2 0.0 copy-start
  48.2 2.0 %collective-permute-done.4.refs_2_ = bf16[2,2,32,256]{3,2,1,0:T(8,128)(2,1)S(1)} collective-permute-done((bf16[2,2,32,256]{3,2,1,0:T(8,128)(2,1)S(1)}, bf16[2,2,32,256]{3,2,1,0:T(8,128)(2,1)S(1)}, u32[]{:S(2)}, u32[]{:S(2)}) %collective-permute-start.4) | collective-permute-done | bytes 65568 | tf_op jit(solution)/shard_map/ppermute | solution.py:178
  50.2 6.4 %all-to-all-done.1.refs_3_ = bf16[4,16,32,256]{3,2,1,0:T(8,128)(2,1)S(1)} async-done(((bf16[4,16,32,256]{3,2,1,0:T(8,128)(2,1)}), bf16[4,16,32,256]{3,2,1,0:T(8,128)(2,1)S(1)}, u32[]{:S(2)}, u32[]{:S(2)}) %all-to-all-start.1) | async-done | bytes 1048608 | tf_op jit(solution)/shard_map/all_to_all | solution.py:190
  56.6 0.0 copy-done
  56.6 2.9 %pair.1 = bf16[16,128,128]{2,1,0:T(8,128)(2,1)} custom-call(bf16[2,32,256]{2,1,0:T(8,128)(2,1)S(1)} %collective-permute-done.2.refs_0_, bf16[2,32,256]{2,1,0:T(8,128)(2,1)S(1)} %collective-permute-done.3.refs_1_, bf16[2,2,32,256]{3,2,1,0:T(8,128)(2,1)S(1)} %collective-permute-done.4.refs_2_, bf16[4,16,32,256]{3,2,1,0:T(8,128)(2,1)S(1)} %all-to-all-done.1.refs_3_, ...), custom_call_target="tpu_custom_call" | custom-call | tf_op jit(solution)/shard_map/pair/pallas_call | solution.py:134
  (5 shorter events, 0.1 us)
Async XLA Ops:
  2.3 9.8 %collective-permute-start = (bf16[2,32,256]{2,1,0:T(8,128)(2,1)}, bf16[2,32,256]{2,1,0:T(8,128)(2,1)S(1)}, u32[]{:S(2)}, u32[]{:S(2)}) collective-permute-start(bf16[2,32,256]{2,1,0:T(8,128)(2,1)} %project.1), channel_id=1, source_target_pairs={{0,4},{1,5},{2,6},{3,7},{4,0},{5,1},{6,2},{7,3},{8,12},{9,13},{10,... | collective-permute-start | bytes 98312 | tf_op jit(solution)/shard_map/ppermute | solution.py:178
  12.2 7.3 %collective-permute-start.1 = (bf16[2,32,256]{2,1,0:T(8,128)(2,1)S(1)}, bf16[2,32,256]{2,1,0:T(8,128)(2,1)S(1)}, u32[]{:S(2)}, u32[]{:S(2)}) collective-permute-start(bf16[2,32,256]{2,1,0:T(8,128)(2,1)S(1)} %pad_maximum_fusion.1), channel_id=1, source_target_pairs={{0,160},{1,161},{2,162},{3,163},{4,256},{5,257},{6,258},{7,259},{8... | collective-permute-start | bytes 98312 | tf_op jit(solution)/shard_map/ppermute | solution.py:178
  20.2 16.7 %all-to-all-start = ((bf16[8,2,32,256]{3,2,1,0:T(8,128)(2,1)}), bf16[8,2,32,256]{3,2,1,0:T(8,128)(2,1)S(1)}, u32[]{:S(2)}, u32[]{:S(2)}) async-start(bf16[8,2,32,256]{3,2,1,0:T(8,128)(2,1)} %broadcast_in_dim.4), calls=%async_computation | async-start | bytes 524288 | tf_op jit(solution)/shard_map/all_to_all | solution.py:184
  26.0 5.9 %collective-permute-start.2 = (bf16[2,32,256]{2,1,0:T(8,128)(2,1)S(1)}, bf16[2,32,256]{2,1,0:T(8,128)(2,1)S(1)}, u32[]{:S(2)}, u32[]{:S(2)}) collective-permute-start(bf16[2,32,256]{2,1,0:T(8,128)(2,1)S(1)} %pad_maximum_fusion.2), channel_id=1, source_target_pairs={{0,24},{1,8},{2,0},{3,16},{4,12},{5,28},{6,20},{7,4},{8,1},{9,17},... | collective-permute-start | bytes 98312 | tf_op jit(solution)/shard_map/ppermute | solution.py:178
  38.0 9.9 %copy-start.1 = (f32[1024,128]{1,0:T(8,128)S(1)}, f32[1024,128]{1,0:T(8,128)}, u32[]{:S(2)}) copy-start(f32[1024,128]{1,0:T(8,128)} %param.16) | copy-start | bytes 1572868
  38.0 18.6 %all-to-all-start.1 = ((bf16[4,16,32,256]{3,2,1,0:T(8,128)(2,1)}), bf16[4,16,32,256]{3,2,1,0:T(8,128)(2,1)S(1)}, u32[]{:S(2)}, u32[]{:S(2)}) async-start(bf16[4,16,32,256]{3,2,1,0:T(8,128)(2,1)} %broadcast_in_dim.5), calls=%async_computation.1 | async-start | bytes 2097152 | tf_op jit(solution)/shard_map/all_to_all | solution.py:190
  41.6 3.1 %collective-permute-start.3 = (bf16[2,32,256]{2,1,0:T(8,128)(2,1)S(1)}, bf16[2,32,256]{2,1,0:T(8,128)(2,1)S(1)}, u32[]{:S(2)}, u32[]{:S(2)}) collective-permute-start(bf16[2,32,256]{2,1,0:T(8,128)(2,1)S(1)} %collective-permute-done.2.refs_0_), channel_id=1, source_target_pairs={{0,4},{1,5},{2,6},{3,7},{4,0},{5,1},{6,2},{7,3},{8,12},{9,13},{10,... | collective-permute-start | bytes 98312 | tf_op jit(solution)/shard_map/ppermute | solution.py:178
  44.8 5.4 %collective-permute-start.4 = (bf16[2,2,32,256]{3,2,1,0:T(8,128)(2,1)S(1)}, bf16[2,2,32,256]{3,2,1,0:T(8,128)(2,1)S(1)}, u32[]{:S(2)}, u32[]{:S(2)}) collective-permute-start(bf16[2,2,32,256]{3,2,1,0:T(8,128)(2,1)S(1)} %pad_maximum_fusion), channel_id=1, source_target_pairs={{0,8},{1,9},{2,10},{3,11},{4,12},{5,13},{6,14},{7,15},{8,0},{9,1},... | collective-permute-start | bytes 196616 | tf_op jit(solution)/shard_map/ppermute | solution.py:178
  48.2 8.4 %copy-start = (f32[128]{0:T(128)S(1)}, f32[128]{0:T(128)}, u32[]{:S(2)}) copy-start(f32[128]{0:T(128)} %param.17) | copy-start | bytes 1540

commit v4 on v3

--- a/solution.py
+++ b/solution.py
@@ -10,6 +10,7 @@
 
 MESH_AXES = ("row", "col", "seq")
 Z_HI, Z_LO, CORES = 2, 4, 2
+SEQ_ORDER = [2, 3, 1, 0]
 BF16, F32 = jnp.bfloat16, jnp.float32
 
 
@@ -80,17 +81,18 @@
 def places():
     col, seq = lax.axis_index("col"), lax.axis_index("seq")
     half = lax.axis_index("row") // (lax.axis_size("row") // Z_HI)
-    per = lax.axis_size("row") // lax.axis_size("col")
+    per, n_y = lax.axis_size("row") // lax.axis_size("col"), lax.axis_size("row") // Z_HI
     z, core = col // CORES, col % CORES
     seqs = []
     for i in (0, 2, 1, 3):
         at = z ^ (core * 2) ^ i ^ seq
-        seqs.append(seq ^ 2 ^ (at % 2 * 3) ^ (at // 2))
+        group = seq ^ 2 ^ (at % 2 * 3) ^ (at // 2)
+        seqs.append(sum(jnp.where(group == s, i, 0) for i, s in enumerate(SEQ_ORDER)))
     blocks = []
     for b in range(per):
         for lo in range(Z_LO):
             for own in range(CORES):
-                blocks.append(home(col, lo, b, half) * 2 + (own ^ half))
+                blocks.append((n_y - 1 - home(col, lo, b, half)) * 2 + (own ^ half))
     return seqs, core, blocks
 
 
@@ -180,14 +182,14 @@
     left, right = (jnp.stack([own[i], other[i]]) for i in range(2))
     right = move(right, lambda r, c, s: (c % CORES * n_y + home(r // per, c // CORES, r % per, c % CORES), r // per, s))
     left = move(left, lambda r, c, s: (r, (left_home(c // CORES, s) ^ c % CORES * 2) * CORES + c % CORES, c // CORES))
-    groups = [list(range(n_y)), list(range(n_y, n_row))]
+    groups = [list(range(n_y))[::-1], list(range(n_y, n_row))[::-1]]
     right = lax.all_to_all(jnp.broadcast_to(right[None], (n_y, *right.shape)), "row", 0, 0, axis_index_groups=groups)
     right = right.reshape(n_row, deep, wide)
     right, left = lax.optimization_barrier((right, left))
     core = move(left, lambda r, c, s: (r, c ^ 1, s))
     near = move(jnp.stack([left, core]), lambda r, c, s: (r, c ^ CORES, s))
     parts = [left, core, near]
-    right = lax.all_to_all(jnp.broadcast_to(right[None], (n_seq, *right.shape)), "seq", 0, 0)
+    right = lax.all_to_all(jnp.broadcast_to(right[None], (n_seq, *right.shape)), "seq", 0, 0, axis_index_groups=[SEQ_ORDER])
     sizes = (n_seq, deep, resid, proj, n_row, n_col // n_seq)
     return pair(sizes, parts, right, w2, b)
 

time: 60 us -> 57.1 us (0.952)
  the two profiles are of different devices: /device:TPU:1 before, /device:TPU:378 now
where the time goes in v4:
time: 57.1 us; the launch traced here: 56.6 us
  waiting for transfers between devices  29.3 us (51%)
  starting transfers between devices  19.1 us (33%)
  Pallas kernels  5.2 us (9%)
  local copies, waits for them, and re-layouts  2.84 us (5%)
    ppermute x5, waiting for transfers between devices, per_device(): lax.ppermute(a, MESH_AXES, [(at(*d), at(*to(*d))) for d in every])  19.2 us
    ppermute x5, starting transfers between devices, per_device(): lax.ppermute(a, MESH_AXES, [(at(*d), at(*to(*d))) for d in every])  9.64 us
    all_to_all x1, waiting for transfers between devices, per_device(): lax.all_to_all(jnp.broadcast_to(right[None], (n_y, *right.shape)), 'row',...  5.21 us
    all_to_all x1, starting transfers between devices, per_device(): lax.all_to_all(jnp.broadcast_to(right[None], (n_seq, *right.shape)), 'seq...  5.11 us
    all_to_all x1, waiting for transfers between devices, per_device(): lax.all_to_all(jnp.broadcast_to(right[None], (n_seq, *right.shape)), 'seq...  4.91 us
    all_to_all x1, starting transfers between devices, per_device(): lax.all_to_all(jnp.broadcast_to(right[None], (n_y, *right.shape)), 'row',...  4.39 us
    pallas_call x1, Pallas kernels, pair(): pl.pallas_call(functools.partial(pair_kernel, sizes), in_specs=[in_vmem]...  2.91 us
    pallas_call x1, Pallas kernels, project(): pl.pallas_call(project_kernel, in_specs=[pl.BlockSpec(memory_space=pltpu....  2.3 us
  transfers between devices with their start and end apart: 7, of which 7 were waited for; matrix products, arithmetic and copies ran while one was open for 2% of the time, Pallas kernels for 0%

profile of v4, /device:TPU:378, one launch (start us, length us, event | category | flops | bytes accessed | tf_op | source)
XLA Modules:
  0.0 56.6 jit_solution(5637691027406329688)
XLA Ops:
  0.0 2.3 %project.1 = bf16[2,32,256]{2,1,0:T(8,128)(2,1)} custom-call(bf16[256,256]{1,0:T(8,128)(2,1)} %bitcast.21, f32[1,256]{1,0:T(1,128)} %bitcast.24, f32[1,256]{1,0:T(1,128)} %bitcast.25, bf16[32,256]{1,0:T(8,128)(2,1)} %bitcast.22, f32[1,32]{1,0:T(1,128)} %bitcast.26, bf16[32,256]{1,0:T(8,128)(2,1)} %bitcast.23, f32[1,32]{1,0:T(1,128)} %bitcast.27), custom_call_target="tpu_custom_call" | custom-call | tf_op jit(solution)/shard_map/project/pallas_call | solution.py:71
  2.3 1.9 %collective-permute-start = (bf16[2,32,256]{2,1,0:T(8,128)(2,1)}, bf16[2,32,256]{2,1,0:T(8,128)(2,1)S(1)}, u32[]{:S(2)}, u32[]{:S(2)}) collective-permute-start(bf16[2,32,256]{2,1,0:T(8,128)(2,1)} %project.1), channel_id=1, source_target_pairs={{0,4},{1,5},{2,6},{3,7},{4,0},{5,1},{6,2},{7,3},{8,12},{9,13},{10,... | collective-permute-start | bytes 98312 | tf_op jit(solution)/shard_map/ppermute | solution.py:180
  4.2 0.7 %fusion = (bf16[1,32,256]{2,1,0:T(8,128)(2,1)S(1)}, bf16[1,32,256]{2,1,0:T(8,128)(2,1)S(1)}) fusion(bf16[2,32,256]{2,1,0:T(8,128)(2,1)} %project.1), kind=kLoop, calls=%fused_computation.4 | loop fusion | bytes 65536 | tf_op jit(solution)/shard_map/slice | solution.py:182
  5.0 0.6 %collective-permute-done = bf16[2,32,256]{2,1,0:T(8,128)(2,1)S(1)} collective-permute-done((bf16[2,32,256]{2,1,0:T(8,128)(2,1)}, bf16[2,32,256]{2,1,0:T(8,128)(2,1)S(1)}, u32[]{:S(2)}, u32[]{:S(2)}) %collective-permute-start) | collective-permute-done | bytes 32800 | tf_op jit(solution)/shard_map/ppermute | solution.py:180
  5.6 1.9 %collective-permute-start.1 = (bf16[2,32,256]{2,1,0:T(8,128)(2,1)S(1)}, bf16[2,32,256]{2,1,0:T(8,128)(2,1)S(1)}, u32[]{:S(2)}, u32[]{:S(2)}) collective-permute-start(bf16[2,32,256]{2,1,0:T(8,128)(2,1)S(1)} %pad_maximum_fusion.1), channel_id=1, source_target_pairs={{0,160},{1,161},{2,162},{3,163},{4,256},{5,257},{6,258},{7,259},{8... | collective-permute-start | bytes 98312 | tf_op jit(solution)/shard_map/ppermute | solution.py:180
  7.6 8.1 %collective-permute-done.1 = bf16[2,32,256]{2,1,0:T(8,128)(2,1)S(1)} collective-permute-done((bf16[2,32,256]{2,1,0:T(8,128)(2,1)S(1)}, bf16[2,32,256]{2,1,0:T(8,128)(2,1)S(1)}, u32[]{:S(2)}, u32[]{:S(2)}) %collective-permute-start.1) | collective-permute-done | bytes 32800 | tf_op jit(solution)/shard_map/ppermute | solution.py:180
  15.7 0.7 %broadcast_in_dim.4 = bf16[8,2,32,256]{3,2,1,0:T(8,128)(2,1)} broadcast(bf16[2,32,256]{2,1,0:T(8,128)(2,1)S(1)} %collective-permute-done.1), dimensions={1,2,3} | broadcast | bytes 294912 | tf_op jit(solution)/shard_map/broadcast_in_dim | solution.py:186
  16.4 4.4 %all-to-all-start = ((bf16[8,2,32,256]{3,2,1,0:T(8,128)(2,1)}), bf16[8,2,32,256]{3,2,1,0:T(8,128)(2,1)S(1)}, u32[]{:S(2)}, u32[]{:S(2)}) async-start(bf16[8,2,32,256]{3,2,1,0:T(8,128)(2,1)} %broadcast_in_dim.4), calls=%async_computation | async-start | bytes 524288 | tf_op jit(solution)/shard_map/all_to_all | solution.py:186
  20.8 1.9 %collective-permute-start.2 = (bf16[2,32,256]{2,1,0:T(8,128)(2,1)S(1)}, bf16[2,32,256]{2,1,0:T(8,128)(2,1)S(1)}, u32[]{:S(2)}, u32[]{:S(2)}) collective-permute-start(bf16[2,32,256]{2,1,0:T(8,128)(2,1)S(1)} %pad_maximum_fusion.2), channel_id=1, source_target_pairs={{0,24},{1,8},{2,0},{3,16},{4,12},{5,28},{6,20},{7,4},{8,1},{9,17},... | collective-permute-start | bytes 98312 | tf_op jit(solution)/shard_map/ppermute | solution.py:180
  22.7 5.4 %collective-permute-done.2.refs_0_ = bf16[2,32,256]{2,1,0:T(8,128)(2,1)S(1)} collective-permute-done((bf16[2,32,256]{2,1,0:T(8,128)(2,1)S(1)}, bf16[2,32,256]{2,1,0:T(8,128)(2,1)S(1)}, u32[]{:S(2)}, u32[]{:S(2)}) %collective-permute-start.2) | collective-permute-done | bytes 32800 | tf_op jit(solution)/shard_map/ppermute | solution.py:180
  28.1 5.2 %all-to-all-done = bf16[8,2,32,256]{3,2,1,0:T(8,128)(2,1)S(1)} async-done(((bf16[8,2,32,256]{3,2,1,0:T(8,128)(2,1)}), bf16[8,2,32,256]{3,2,1,0:T(8,128)(2,1)S(1)}, u32[]{:S(2)}, u32[]{:S(2)}) %all-to-all-start) | async-done | bytes 262176 | tf_op jit(solution)/shard_map/all_to_all | solution.py:186
  33.3 1.1 %broadcast_in_dim.5 = bf16[4,16,32,256]{3,2,1,0:T(8,128)(2,1)} broadcast(bf16[16,32,256]{2,1,0:T(8,128)(2,1)S(1)} %bitcast.18), dimensions={1,2,3} | broadcast | bytes 1310720 | tf_op jit(solution)/shard_map/broadcast_in_dim | solution.py:192
  34.4 0.0 copy-start.1
  34.4 5.1 %all-to-all-start.1 = ((bf16[4,16,32,256]{3,2,1,0:T(8,128)(2,1)}), bf16[4,16,32,256]{3,2,1,0:T(8,128)(2,1)S(1)}, u32[]{:S(2)}, u32[]{:S(2)}) async-start(bf16[4,16,32,256]{3,2,1,0:T(8,128)(2,1)} %broadcast_in_dim.5), calls=%async_computation.1 | async-start | bytes 2097152 | tf_op jit(solution)/shard_map/all_to_all | solution.py:192
  39.5 1.9 %collective-permute-start.3 = (bf16[2,32,256]{2,1,0:T(8,128)(2,1)S(1)}, bf16[2,32,256]{2,1,0:T(8,128)(2,1)S(1)}, u32[]{:S(2)}, u32[]{:S(2)}) collective-permute-start(bf16[2,32,256]{2,1,0:T(8,128)(2,1)S(1)} %collective-permute-done.2.refs_0_), channel_id=1, source_target_pairs={{0,4},{1,5},{2,6},{3,7},{4,0},{5,1},{6,2},{7,3},{8,12},{9,13},{10,... | collective-permute-start | bytes 98312 | tf_op jit(solution)/shard_map/ppermute | solution.py:180
  41.5 1.2 %collective-permute-done.3.refs_1_ = bf16[2,32,256]{2,1,0:T(8,128)(2,1)S(1)} collective-permute-done((bf16[2,32,256]{2,1,0:T(8,128)(2,1)S(1)}, bf16[2,32,256]{2,1,0:T(8,128)(2,1)S(1)}, u32[]{:S(2)}, u32[]{:S(2)}) %collective-permute-start.3) | collective-permute-done | bytes 32800 | tf_op jit(solution)/shard_map/ppermute | solution.py:180
  42.6 2.0 %collective-permute-start.4 = (bf16[2,2,32,256]{3,2,1,0:T(8,128)(2,1)S(1)}, bf16[2,2,32,256]{3,2,1,0:T(8,128)(2,1)S(1)}, u32[]{:S(2)}, u32[]{:S(2)}) collective-permute-start(bf16[2,2,32,256]{3,2,1,0:T(8,128)(2,1)S(1)} %pad_maximum_fusion), channel_id=1, source_target_pairs={{0,8},{1,9},{2,10},{3,11},{4,12},{5,13},{6,14},{7,15},{8,0},{9,1},... | collective-permute-start | bytes 196616 | tf_op jit(solution)/shard_map/ppermute | solution.py:180
  44.6 0.0 copy-done.1
  44.7 0.1 copy.12
  44.8 0.1 copy.13.refs_4_
  44.9 0.0 copy-start
  44.9 3.9 %collective-permute-done.4.refs_2_ = bf16[2,2,32,256]{3,2,1,0:T(8,128)(2,1)S(1)} collective-permute-done((bf16[2,2,32,256]{3,2,1,0:T(8,128)(2,1)S(1)}, bf16[2,2,32,256]{3,2,1,0:T(8,128)(2,1)S(1)}, u32[]{:S(2)}, u32[]{:S(2)}) %collective-permute-start.4) | collective-permute-done | bytes 65568 | tf_op jit(solution)/shard_map/ppermute | solution.py:180
  48.8 4.9 %all-to-all-done.1.refs_3_ = bf16[4,16,32,256]{3,2,1,0:T(8,128)(2,1)S(1)} async-done(((bf16[4,16,32,256]{3,2,1,0:T(8,128)(2,1)}), bf16[4,16,32,256]{3,2,1,0:T(8,128)(2,1)S(1)}, u32[]{:S(2)}, u32[]{:S(2)}) %all-to-all-start.1) | async-done | bytes 1048608 | tf_op jit(solution)/shard_map/all_to_all | solution.py:192
  53.7 0.0 copy-done
  53.7 2.9 %pair.1 = bf16[16,128,128]{2,1,0:T(8,128)(2,1)} custom-call(bf16[2,32,256]{2,1,0:T(8,128)(2,1)S(1)} %collective-permute-done.2.refs_0_, bf16[2,32,256]{2,1,0:T(8,128)(2,1)S(1)} %collective-permute-done.3.refs_1_, bf16[2,2,32,256]{3,2,1,0:T(8,128)(2,1)S(1)} %collective-permute-done.4.refs_2_, bf16[4,16,32,256]{3,2,1,0:T(8,128)(2,1)S(1)} %all-to-all-done.1.refs_3_, ...), custom_call_target="tpu_custom_call" | custom-call | tf_op jit(solution)/shard_map/pair/pallas_call | solution.py:136
  (5 shorter events, 0.1 us)
Async XLA Ops:
  2.3 3.3 %collective-permute-start = (bf16[2,32,256]{2,1,0:T(8,128)(2,1)}, bf16[2,32,256]{2,1,0:T(8,128)(2,1)S(1)}, u32[]{:S(2)}, u32[]{:S(2)}) collective-permute-start(bf16[2,32,256]{2,1,0:T(8,128)(2,1)} %project.1), channel_id=1, source_target_pairs={{0,4},{1,5},{2,6},{3,7},{4,0},{5,1},{6,2},{7,3},{8,12},{9,13},{10,... | collective-permute-start | bytes 98312 | tf_op jit(solution)/shard_map/ppermute | solution.py:180
  5.6 10.0 %collective-permute-start.1 = (bf16[2,32,256]{2,1,0:T(8,128)(2,1)S(1)}, bf16[2,32,256]{2,1,0:T(8,128)(2,1)S(1)}, u32[]{:S(2)}, u32[]{:S(2)}) collective-permute-start(bf16[2,32,256]{2,1,0:T(8,128)(2,1)S(1)} %pad_maximum_fusion.1), channel_id=1, source_target_pairs={{0,160},{1,161},{2,162},{3,163},{4,256},{5,257},{6,258},{7,259},{8... | collective-permute-start | bytes 98312 | tf_op jit(solution)/shard_map/ppermute | solution.py:180
  16.4 16.9 %all-to-all-start = ((bf16[8,2,32,256]{3,2,1,0:T(8,128)(2,1)}), bf16[8,2,32,256]{3,2,1,0:T(8,128)(2,1)S(1)}, u32[]{:S(2)}, u32[]{:S(2)}) async-start(bf16[8,2,32,256]{3,2,1,0:T(8,128)(2,1)} %broadcast_in_dim.4), calls=%async_computation | async-start | bytes 524288 | tf_op jit(solution)/shard_map/all_to_all | solution.py:186
  20.8 7.3 %collective-permute-start.2 = (bf16[2,32,256]{2,1,0:T(8,128)(2,1)S(1)}, bf16[2,32,256]{2,1,0:T(8,128)(2,1)S(1)}, u32[]{:S(2)}, u32[]{:S(2)}) collective-permute-start(bf16[2,32,256]{2,1,0:T(8,128)(2,1)S(1)} %pad_maximum_fusion.2), channel_id=1, source_target_pairs={{0,24},{1,8},{2,0},{3,16},{4,12},{5,28},{6,20},{7,4},{8,1},{9,17},... | collective-permute-start | bytes 98312 | tf_op jit(solution)/shard_map/ppermute | solution.py:180
  34.4 10.2 %copy-start.1 = (f32[1024,128]{1,0:T(8,128)S(1)}, f32[1024,128]{1,0:T(8,128)}, u32[]{:S(2)}) copy-start(f32[1024,128]{1,0:T(8,128)} %param.16) | copy-start | bytes 1572868
  34.4 19.3 %all-to-all-start.1 = ((bf16[4,16,32,256]{3,2,1,0:T(8,128)(2,1)}), bf16[4,16,32,256]{3,2,1,0:T(8,128)(2,1)S(1)}, u32[]{:S(2)}, u32[]{:S(2)}) async-start(bf16[4,16,32,256]{3,2,1,0:T(8,128)(2,1)} %broadcast_in_dim.5), calls=%async_computation.1 | async-start | bytes 2097152 | tf_op jit(solution)/shard_map/all_to_all | solution.py:192
  39.5 3.1 %collective-permute-start.3 = (bf16[2,32,256]{2,1,0:T(8,128)(2,1)S(1)}, bf16[2,32,256]{2,1,0:T(8,128)(2,1)S(1)}, u32[]{:S(2)}, u32[]{:S(2)}) collective-permute-start(bf16[2,32,256]{2,1,0:T(8,128)(2,1)S(1)} %collective-permute-done.2.refs_0_), channel_id=1, source_target_pairs={{0,4},{1,5},{2,6},{3,7},{4,0},{5,1},{6,2},{7,3},{8,12},{9,13},{10,... | collective-permute-start | bytes 98312 | tf_op jit(solution)/shard_map/ppermute | solution.py:180
  42.6 6.2 %collective-permute-start.4 = (bf16[2,2,32,256]{3,2,1,0:T(8,128)(2,1)S(1)}, bf16[2,2,32,256]{3,2,1,0:T(8,128)(2,1)S(1)}, u32[]{:S(2)}, u32[]{:S(2)}) collective-permute-start(bf16[2,2,32,256]{3,2,1,0:T(8,128)(2,1)S(1)} %pad_maximum_fusion), channel_id=1, source_target_pairs={{0,8},{1,9},{2,10},{3,11},{4,12},{5,13},{6,14},{7,15},{8,0},{9,1},... | collective-permute-start | bytes 196616 | tf_op jit(solution)/shard_map/ppermute | solution.py:180
  44.9 8.8 %copy-start = (f32[128]{0:T(128)S(1)}, f32[128]{0:T(128)}, u32[]{:S(2)}) copy-start(f32[128]{0:T(128)} %param.17) | copy-start | bytes 1540

commit v5 on v4

--- a/solution.py
+++ b/solution.py
@@ -96,19 +96,35 @@
     return seqs, core, blocks
 
 
+def turn_kernel(own_ref, core_ref, near_ref, out_ref):
+    core, lanes = lax.axis_index("col") % CORES, 128
+    halves = own_ref.shape[-1] // lanes
+    refs = [own_ref, core_ref, near_ref.at[0], near_ref.at[1]]
+    for ib in range(own_ref.shape[0]):
+        for h in range(halves):
+            own = [ref[ib ^ core ^ i % CORES, :, h * lanes : (h + 1) * lanes] for i, ref in enumerate(refs)]
+            out_ref[pl.ds((ib * halves + h) * lanes, lanes), :] = jnp.concatenate(own).astype(F32).T.astype(BF16)
+
+
+def turn(parts):
+    blocks, deep, wide = parts[0].shape
+    return pl.pallas_call(
+        turn_kernel,
+        out_shape=jax.ShapeDtypeStruct((blocks * wide, Z_LO * deep), BF16),
+        compiler_params=pltpu.CompilerParams(vmem_limit_bytes=16 * 1024 * 1024),
+        cost_estimate=pl.CostEstimate(flops=0, bytes_accessed=2**18, transcendentals=0),
+        name="turn",
+    )(*parts)
+
+
 def pair_kernel(sizes, *refs):
     n_seq, deep, resid, proj, jblocks, iblocks = sizes
-    own_ref, core_ref, near_ref, right_ref, w_ref, b_ref, out_ref, lt, rt, outer = refs
-    left_refs = [own_ref, core_ref, near_ref.at[0], near_ref.at[1]]
-    seqs, core, blocks = places()
+    lt, right_ref, w_ref, b_ref, out_ref, rt, outer, done, sems = refs
+    seqs, _, blocks = places()
     depth, lanes = n_seq * deep, 128
     per_r = lanes // resid
     halves = resid * proj // lanes
     n_i, cols = iblocks * resid, jblocks * resid
-    for ib in range(iblocks):
-        for h in range(halves):
-            own = [ref[ib ^ core ^ i % CORES, :, h * lanes : (h + 1) * lanes] for i, ref in enumerate(left_refs)]
-            lt[pl.ds((ib * halves + h) * lanes, lanes), :] = jnp.concatenate(own).astype(F32).T.astype(BF16)
     for jb in range(jblocks):
         at = blocks[jb]
         for h in range(halves):
@@ -122,29 +138,37 @@
             outer[:, pl.ds((p * 2 + q) * proj, proj), :] = o[:, q * cols : (q + 1) * cols].reshape(n_i, proj, cols)
     w = w_ref[...]
     bias = b_ref[...]
+    copies = []
     for p in range(n_i // 2):
         rhs = jnp.concatenate([outer[p * 2], outer[p * 2 + 1]], axis=1)
         res = jnp.dot(w, rhs, preferred_element_type=F32)
         for q in range(2):
-            out_ref[p * 2 + q] = (res[:, q * cols : (q + 1) * cols].T + bias).astype(BF16)
-
-
-def pair(sizes, parts, right, w2, bias):
+            done[p * 2 + q] = (res[:, q * cols : (q + 1) * cols].T + bias).astype(BF16)
+        rows = pl.ds(p * 2, 2)
+        copies.append(pltpu.make_async_copy(done.at[rows], out_ref.at[rows], sems.at[p]))
+        copies[-1].start()
+    for copy in copies:
+        copy.wait()
+
+
+def pair(sizes, left, right, w2, bias):
     n_seq, deep, resid, proj, jblocks, iblocks = sizes
     n_i, n_j, cz = iblocks * resid, jblocks * resid, w2.shape[0]
     in_vmem = pl.BlockSpec(memory_space=pltpu.VMEM)
     return pl.pallas_call(
         functools.partial(pair_kernel, sizes),
-        in_specs=[in_vmem] * (len(parts) + 3),
+        in_specs=[in_vmem] * 4,
+        out_specs=pl.BlockSpec(memory_space=pl.ANY),
         out_shape=jax.ShapeDtypeStruct((n_i, n_j, cz), BF16),
         scratch_shapes=[
-            pltpu.VMEM((n_i * proj, n_seq * deep), BF16),
             pltpu.VMEM((proj, n_j, n_seq * deep), F32),
             pltpu.VMEM((n_i, proj * proj, n_j), BF16),
+            pltpu.VMEM((n_i, n_j, cz), BF16),
+            pltpu.SemaphoreType.DMA((n_i // 2,)),
         ],
         compiler_params=pltpu.CompilerParams(vmem_limit_bytes=48 * 1024 * 1024),
         name="pair",
-    )(*parts, right, w2, bias.reshape(1, -1))
+    )(left, right, w2, bias.reshape(1, -1))
 
 
 def spread_weight(w, proj, inv):
@@ -191,7 +215,7 @@
     parts = [left, core, near]
     right = lax.all_to_all(jnp.broadcast_to(right[None], (n_seq, *right.shape)), "seq", 0, 0, axis_index_groups=[SEQ_ORDER])
     sizes = (n_seq, deep, resid, proj, n_row, n_col // n_seq)
-    return pair(sizes, parts, right, w2, b)
+    return pair(sizes, turn(parts), right, w2, b)
 
 
 def solution(mesh):

time: 57.1 us -> 57 us (level)
  no operation moved by 1% of the time
where the time goes in v5:
time: 57 us; the launch traced here: 56.5 us
  waiting for transfers between devices  29.2 us (51%)
  starting transfers between devices  19.1 us (34%)
  Pallas kernels  5.17 us (9%)
  local copies, waits for them, and re-layouts  2.84 us (5%)
    ppermute x5, waiting for transfers between devices, per_device(): lax.ppermute(a, MESH_AXES, [(at(*d), at(*to(*d))) for d in every])  19.2 us
    ppermute x5, starting transfers between devices, per_device(): lax.ppermute(a, MESH_AXES, [(at(*d), at(*to(*d))) for d in every])  9.64 us
    all_to_all x1, waiting for transfers between devices, per_device(): lax.all_to_all(jnp.broadcast_to(right[None], (n_y, *right.shape)), 'row',...  5.21 us
    all_to_all x1, starting transfers between devices, per_device(): lax.all_to_all(jnp.broadcast_to(right[None], (n_seq, *right.shape)), 'seq...  5.11 us
    all_to_all x1, waiting for transfers between devices, per_device(): lax.all_to_all(jnp.broadcast_to(right[None], (n_seq, *right.shape)), 'seq...  4.79 us
    all_to_all x1, starting transfers between devices, per_device(): lax.all_to_all(jnp.broadcast_to(right[None], (n_y, *right.shape)), 'row',...  4.39 us
    pallas_call x1, Pallas kernels, pair(): pl.pallas_call(functools.partial(pair_kernel, sizes), in_specs=[in_vmem]...  2.77 us
    pallas_call x1, Pallas kernels, project(): pl.pallas_call(project_kernel, in_specs=[pl.BlockSpec(memory_space=pltpu....  2.3 us
  transfers between devices with their start and end apart: 7, of which 7 were waited for; matrix products, arithmetic and copies ran while one was open for 2% of the time, Pallas kernels for 0%

profile of v5, /device:TPU:378, one launch (start us, length us, event | category | flops | bytes accessed | tf_op | source)
XLA Modules:
  0.0 56.5 jit_solution(16317192167385598525)
XLA Ops:
  0.0 2.3 %project.1 = bf16[2,32,256]{2,1,0:T(8,128)(2,1)} custom-call(bf16[256,256]{1,0:T(8,128)(2,1)} %bitcast.21, f32[1,256]{1,0:T(1,128)} %bitcast.24, f32[1,256]{1,0:T(1,128)} %bitcast.25, bf16[32,256]{1,0:T(8,128)(2,1)} %bitcast.22, f32[1,32]{1,0:T(1,128)} %bitcast.26, bf16[32,256]{1,0:T(8,128)(2,1)} %bitcast.23, f32[1,32]{1,0:T(1,128)} %bitcast.27), custom_call_target="tpu_custom_call" | custom-call | tf_op jit(solution)/shard_map/project/pallas_call | solution.py:71
  2.3 1.9 %collective-permute-start = (bf16[2,32,256]{2,1,0:T(8,128)(2,1)}, bf16[2,32,256]{2,1,0:T(8,128)(2,1)S(1)}, u32[]{:S(2)}, u32[]{:S(2)}) collective-permute-start(bf16[2,32,256]{2,1,0:T(8,128)(2,1)} %project.1), channel_id=1, source_target_pairs={{0,4},{1,5},{2,6},{3,7},{4,0},{5,1},{6,2},{7,3},{8,12},{9,13},{10,... | collective-permute-start | bytes 98312 | tf_op jit(solution)/shard_map/ppermute | solution.py:204
  4.2 0.7 %fusion = (bf16[1,32,256]{2,1,0:T(8,128)(2,1)S(1)}, bf16[1,32,256]{2,1,0:T(8,128)(2,1)S(1)}) fusion(bf16[2,32,256]{2,1,0:T(8,128)(2,1)} %project.1), kind=kLoop, calls=%fused_computation.4 | loop fusion | bytes 65536 | tf_op jit(solution)/shard_map/slice | solution.py:206
  5.0 0.6 %collective-permute-done = bf16[2,32,256]{2,1,0:T(8,128)(2,1)S(1)} collective-permute-done((bf16[2,32,256]{2,1,0:T(8,128)(2,1)}, bf16[2,32,256]{2,1,0:T(8,128)(2,1)S(1)}, u32[]{:S(2)}, u32[]{:S(2)}) %collective-permute-start) | collective-permute-done | bytes 32800 | tf_op jit(solution)/shard_map/ppermute | solution.py:204
  5.6 1.9 %collective-permute-start.1 = (bf16[2,32,256]{2,1,0:T(8,128)(2,1)S(1)}, bf16[2,32,256]{2,1,0:T(8,128)(2,1)S(1)}, u32[]{:S(2)}, u32[]{:S(2)}) collective-permute-start(bf16[2,32,256]{2,1,0:T(8,128)(2,1)S(1)} %pad_maximum_fusion.1), channel_id=1, source_target_pairs={{0,160},{1,161},{2,162},{3,163},{4,256},{5,257},{6,258},{7,259},{8... | collective-permute-start | bytes 98312 | tf_op jit(solution)/shard_map/ppermute | solution.py:204
  7.6 8.1 %collective-permute-done.1 = bf16[2,32,256]{2,1,0:T(8,128)(2,1)S(1)} collective-permute-done((bf16[2,32,256]{2,1,0:T(8,128)(2,1)S(1)}, bf16[2,32,256]{2,1,0:T(8,128)(2,1)S(1)}, u32[]{:S(2)}, u32[]{:S(2)}) %collective-permute-start.1) | collective-permute-done | bytes 32800 | tf_op jit(solution)/shard_map/ppermute | solution.py:204
  15.7 0.7 %broadcast_in_dim.4 = bf16[8,2,32,256]{3,2,1,0:T(8,128)(2,1)} broadcast(bf16[2,32,256]{2,1,0:T(8,128)(2,1)S(1)} %collective-permute-done.1), dimensions={1,2,3} | broadcast | bytes 294912 | tf_op jit(solution)/shard_map/broadcast_in_dim | solution.py:210
  16.4 4.4 %all-to-all-start = ((bf16[8,2,32,256]{3,2,1,0:T(8,128)(2,1)}), bf16[8,2,32,256]{3,2,1,0:T(8,128)(2,1)S(1)}, u32[]{:S(2)}, u32[]{:S(2)}) async-start(bf16[8,2,32,256]{3,2,1,0:T(8,128)(2,1)} %broadcast_in_dim.4), calls=%async_computation | async-start | bytes 524288 | tf_op jit(solution)/shard_map/all_to_all | solution.py:210
  20.8 1.9 %collective-permute-start.2 = (bf16[2,32,256]{2,1,0:T(8,128)(2,1)S(1)}, bf16[2,32,256]{2,1,0:T(8,128)(2,1)S(1)}, u32[]{:S(2)}, u32[]{:S(2)}) collective-permute-start(bf16[2,32,256]{2,1,0:T(8,128)(2,1)S(1)} %pad_maximum_fusion.2), channel_id=1, source_target_pairs={{0,24},{1,8},{2,0},{3,16},{4,12},{5,28},{6,20},{7,4},{8,1},{9,17},... | collective-permute-start | bytes 98312 | tf_op jit(solution)/shard_map/ppermute | solution.py:204
  22.7 5.4 %collective-permute-done.2.own_ref = bf16[2,32,256]{2,1,0:T(8,128)(2,1)S(1)} collective-permute-done((bf16[2,32,256]{2,1,0:T(8,128)(2,1)S(1)}, bf16[2,32,256]{2,1,0:T(8,128)(2,1)S(1)}, u32[]{:S(2)}, u32[]{:S(2)}) %collective-permute-start.2) | collective-permute-done | bytes 32800 | tf_op jit(solution)/shard_map/ppermute | solution.py:204
  28.1 5.2 %all-to-all-done = bf16[8,2,32,256]{3,2,1,0:T(8,128)(2,1)S(1)} async-done(((bf16[8,2,32,256]{3,2,1,0:T(8,128)(2,1)}), bf16[8,2,32,256]{3,2,1,0:T(8,128)(2,1)S(1)}, u32[]{:S(2)}, u32[]{:S(2)}) %all-to-all-start) | async-done | bytes 262176 | tf_op jit(solution)/shard_map/all_to_all | solution.py:210
  33.3 1.1 %broadcast_in_dim.5 = bf16[4,16,32,256]{3,2,1,0:T(8,128)(2,1)} broadcast(bf16[16,32,256]{2,1,0:T(8,128)(2,1)S(1)} %bitcast.18), dimensions={1,2,3} | broadcast | bytes 1310720 | tf_op jit(solution)/shard_map/broadcast_in_dim | solution.py:216
  34.4 0.0 copy-start.1
  34.4 5.1 %all-to-all-start.1 = ((bf16[4,16,32,256]{3,2,1,0:T(8,128)(2,1)}), bf16[4,16,32,256]{3,2,1,0:T(8,128)(2,1)S(1)}, u32[]{:S(2)}, u32[]{:S(2)}) async-start(bf16[4,16,32,256]{3,2,1,0:T(8,128)(2,1)} %broadcast_in_dim.5), calls=%async_computation.1 | async-start | bytes 2097152 | tf_op jit(solution)/shard_map/all_to_all | solution.py:216
  39.5 1.9 %collective-permute-start.3 = (bf16[2,32,256]{2,1,0:T(8,128)(2,1)S(1)}, bf16[2,32,256]{2,1,0:T(8,128)(2,1)S(1)}, u32[]{:S(2)}, u32[]{:S(2)}) collective-permute-start(bf16[2,32,256]{2,1,0:T(8,128)(2,1)S(1)} %collective-permute-done.2.own_ref), channel_id=1, source_target_pairs={{0,4},{1,5},{2,6},{3,7},{4,0},{5,1},{6,2},{7,3},{8,12},{9,13},{10,... | collective-permute-start | bytes 98312 | tf_op jit(solution)/shard_map/ppermute | solution.py:204
  41.5 1.2 %collective-permute-done.3.core_ref = bf16[2,32,256]{2,1,0:T(8,128)(2,1)S(1)} collective-permute-done((bf16[2,32,256]{2,1,0:T(8,128)(2,1)S(1)}, bf16[2,32,256]{2,1,0:T(8,128)(2,1)S(1)}, u32[]{:S(2)}, u32[]{:S(2)}) %collective-permute-start.3) | collective-permute-done | bytes 32800 | tf_op jit(solution)/shard_map/ppermute | solution.py:204
  42.6 2.0 %collective-permute-start.4 = (bf16[2,2,32,256]{3,2,1,0:T(8,128)(2,1)S(1)}, bf16[2,2,32,256]{3,2,1,0:T(8,128)(2,1)S(1)}, u32[]{:S(2)}, u32[]{:S(2)}) collective-permute-start(bf16[2,2,32,256]{3,2,1,0:T(8,128)(2,1)S(1)} %pad_maximum_fusion), channel_id=1, source_target_pairs={{0,8},{1,9},{2,10},{3,11},{4,12},{5,13},{6,14},{7,15},{8,0},{9,1},... | collective-permute-start | bytes 196616 | tf_op jit(solution)/shard_map/ppermute | solution.py:204
  44.6 0.0 copy-done.1
  44.7 0.1 copy.12
  44.8 0.1 copy.13.refs_2_
  44.9 3.9 %collective-permute-done.4.near_ref = bf16[2,2,32,256]{3,2,1,0:T(8,128)(2,1)S(1)} collective-permute-done((bf16[2,2,32,256]{3,2,1,0:T(8,128)(2,1)S(1)}, bf16[2,2,32,256]{3,2,1,0:T(8,128)(2,1)S(1)}, u32[]{:S(2)}, u32[]{:S(2)}) %collective-permute-start.4) | collective-permute-done | bytes 65568 | tf_op jit(solution)/shard_map/ppermute | solution.py:204
  48.8 0.1 turn.1.refs_0_
  48.9 0.0 copy-start
  48.9 4.8 %all-to-all-done.1.refs_1_ = bf16[4,16,32,256]{3,2,1,0:T(8,128)(2,1)S(1)} async-done(((bf16[4,16,32,256]{3,2,1,0:T(8,128)(2,1)}), bf16[4,16,32,256]{3,2,1,0:T(8,128)(2,1)S(1)}, u32[]{:S(2)}, u32[]{:S(2)}) %all-to-all-start.1) | async-done | bytes 1048608 | tf_op jit(solution)/shard_map/all_to_all | solution.py:216
  53.7 0.0 copy-done
  53.7 2.8 %pair.1 = bf16[16,128,128]{2,1,0:T(8,128)(2,1)} custom-call(bf16[512,128]{1,0:T(8,128)(2,1)S(1)} %turn.1.refs_0_, bf16[4,16,32,256]{3,2,1,0:T(8,128)(2,1)S(1)} %all-to-all-done.1.refs_1_, bf16[128,1024]{1,0:T(8,128)(2,1)S(1)} %copy.13.refs_2_, f32[1,128]{1,0:T(1,128)S(1)} %bitcast.17), custom_call_target="tpu_custom_call" | custom-call | tf_op jit(solution)/shard_map/pair/pallas_call | solution.py:158
  (5 shorter events, 0.1 us)
Async XLA Ops:
  2.3 3.3 %collective-permute-start = (bf16[2,32,256]{2,1,0:T(8,128)(2,1)}, bf16[2,32,256]{2,1,0:T(8,128)(2,1)S(1)}, u32[]{:S(2)}, u32[]{:S(2)}) collective-permute-start(bf16[2,32,256]{2,1,0:T(8,128)(2,1)} %project.1), channel_id=1, source_target_pairs={{0,4},{1,5},{2,6},{3,7},{4,0},{5,1},{6,2},{7,3},{8,12},{9,13},{10,... | collective-permute-start | bytes 98312 | tf_op jit(solution)/shard_map/ppermute | solution.py:204
  5.6 10.0 %collective-permute-start.1 = (bf16[2,32,256]{2,1,0:T(8,128)(2,1)S(1)}, bf16[2,32,256]{2,1,0:T(8,128)(2,1)S(1)}, u32[]{:S(2)}, u32[]{:S(2)}) collective-permute-start(bf16[2,32,256]{2,1,0:T(8,128)(2,1)S(1)} %pad_maximum_fusion.1), channel_id=1, source_target_pairs={{0,160},{1,161},{2,162},{3,163},{4,256},{5,257},{6,258},{7,259},{8... | collective-permute-start | bytes 98312 | tf_op jit(solution)/shard_map/ppermute | solution.py:204
  16.4 16.9 %all-to-all-start = ((bf16[8,2,32,256]{3,2,1,0:T(8,128)(2,1)}), bf16[8,2,32,256]{3,2,1,0:T(8,128)(2,1)S(1)}, u32[]{:S(2)}, u32[]{:S(2)}) async-start(bf16[8,2,32,256]{3,2,1,0:T(8,128)(2,1)} %broadcast_in_dim.4), calls=%async_computation | async-start | bytes 524288 | tf_op jit(solution)/shard_map/all_to_all | solution.py:210
  20.8 7.3 %collective-permute-start.2 = (bf16[2,32,256]{2,1,0:T(8,128)(2,1)S(1)}, bf16[2,32,256]{2,1,0:T(8,128)(2,1)S(1)}, u32[]{:S(2)}, u32[]{:S(2)}) collective-permute-start(bf16[2,32,256]{2,1,0:T(8,128)(2,1)S(1)} %pad_maximum_fusion.2), channel_id=1, source_target_pairs={{0,24},{1,8},{2,0},{3,16},{4,12},{5,28},{6,20},{7,4},{8,1},{9,17},... | collective-permute-start | bytes 98312 | tf_op jit(solution)/shard_map/ppermute | solution.py:204
  34.4 10.2 %copy-start.1 = (f32[1024,128]{1,0:T(8,128)S(1)}, f32[1024,128]{1,0:T(8,128)}, u32[]{:S(2)}) copy-start(f32[1024,128]{1,0:T(8,128)} %param.16) | copy-start | bytes 1572868
  34.4 19.3 %all-to-all-start.1 = ((bf16[4,16,32,256]{3,2,1,0:T(8,128)(2,1)}), bf16[4,16,32,256]{3,2,1,0:T(8,128)(2,1)S(1)}, u32[]{:S(2)}, u32[]{:S(2)}) async-start(bf16[4,16,32,256]{3,2,1,0:T(8,128)(2,1)} %broadcast_in_dim.5), calls=%async_computation.1 | async-start | bytes 2097152 | tf_op jit(solution)/shard_map/all_to_all | solution.py:216
  39.5 3.1 %collective-permute-start.3 = (bf16[2,32,256]{2,1,0:T(8,128)(2,1)S(1)}, bf16[2,32,256]{2,1,0:T(8,128)(2,1)S(1)}, u32[]{:S(2)}, u32[]{:S(2)}) collective-permute-start(bf16[2,32,256]{2,1,0:T(8,128)(2,1)S(1)} %collective-permute-done.2.own_ref), channel_id=1, source_target_pairs={{0,4},{1,5},{2,6},{3,7},{4,0},{5,1},{6,2},{7,3},{8,12},{9,13},{10,... | collective-permute-start | bytes 98312 | tf_op jit(solution)/shard_map/ppermute | solution.py:204
  42.6 6.2 %collective-permute-start.4 = (bf16[2,2,32,256]{3,2,1,0:T(8,128)(2,1)S(1)}, bf16[2,2,32,256]{3,2,1,0:T(8,128)(2,1)S(1)}, u32[]{:S(2)}, u32[]{:S(2)}) collective-permute-start(bf16[2,2,32,256]{3,2,1,0:T(8,128)(2,1)S(1)} %pad_maximum_fusion), channel_id=1, source_target_pairs={{0,8},{1,9},{2,10},{3,11},{4,12},{5,13},{6,14},{7,15},{8,0},{9,1},... | collective-permute-start | bytes 196616 | tf_op jit(solution)/shard_map/ppermute | solution.py:204
  48.9 4.8 %copy-start = (f32[128]{0:T(128)S(1)}, f32[128]{0:T(128)}, u32[]{:S(2)}) copy-start(f32[128]{0:T(128)} %param.17) | copy-start | bytes 1540

commit v6 on v5

--- a/solution.py
+++ b/solution.py
@@ -10,6 +10,7 @@
 
 MESH_AXES = ("row", "col", "seq")
 Z_HI, Z_LO, CORES = 2, 4, 2
+Y_ORDER = [7, 6, 5, 4, 3, 2, 0, 1]
 SEQ_ORDER = [2, 3, 1, 0]
 BF16, F32 = jnp.bfloat16, jnp.float32
 
@@ -81,7 +82,7 @@
 def places():
     col, seq = lax.axis_index("col"), lax.axis_index("seq")
     half = lax.axis_index("row") // (lax.axis_size("row") // Z_HI)
-    per, n_y = lax.axis_size("row") // lax.axis_size("col"), lax.axis_size("row") // Z_HI
+    per = lax.axis_size("row") // lax.axis_size("col")
     z, core = col // CORES, col % CORES
     seqs = []
     for i in (0, 2, 1, 3):
@@ -92,7 +93,8 @@
     for b in range(per):
         for lo in range(Z_LO):
             for own in range(CORES):
-                blocks.append((n_y - 1 - home(col, lo, b, half)) * 2 + (own ^ half))
+                y = home(col, lo, b, half)
+                blocks.append(sum(jnp.where(y == a, i, 0) for i, a in enumerate(Y_ORDER)) * 2 + (own ^ half))
     return seqs, core, blocks
 
 
@@ -206,7 +208,7 @@
     left, right = (jnp.stack([own[i], other[i]]) for i in range(2))
     right = move(right, lambda r, c, s: (c % CORES * n_y + home(r // per, c // CORES, r % per, c % CORES), r // per, s))
     left = move(left, lambda r, c, s: (r, (left_home(c // CORES, s) ^ c % CORES * 2) * CORES + c % CORES, c // CORES))
-    groups = [list(range(n_y))[::-1], list(range(n_y, n_row))[::-1]]
+    groups = [[half * n_y + y for y in Y_ORDER] for half in range(Z_HI)]
     right = lax.all_to_all(jnp.broadcast_to(right[None], (n_y, *right.shape)), "row", 0, 0, axis_index_groups=groups)
     right = right.reshape(n_row, deep, wide)
     right, left = lax.optimization_barrier((right, left))

time: 57 us -> 56.9 us (level)
  the two profiles are of different devices: /device:TPU:378 before, /device:TPU:2 now
where the time goes in v6:
time: 56.9 us; the launch traced here: 56.4 us
  starting transfers between devices  34 us (60%)
  waiting for transfers between devices  14.2 us (25%)
  Pallas kernels  5.2 us (9%)
  local copies, waits for them, and re-layouts  2.84 us (5%)
    ppermute x5, starting transfers between devices, per_device(): lax.ppermute(a, MESH_AXES, [(at(*d), at(*to(*d))) for d in every])  17.6 us
    ppermute x5, waiting for transfers between devices, per_device(): lax.ppermute(a, MESH_AXES, [(at(*d), at(*to(*d))) for d in every])  10.3 us
    all_to_all x1, starting transfers between devices, per_device(): lax.all_to_all(jnp.broadcast_to(right[None], (n_seq, *right.shape)), 'seq...  9.65 us
    all_to_all x1, starting transfers between devices, per_device(): lax.all_to_all(jnp.broadcast_to(right[None], (n_y, *right.shape)), 'row',...  6.7 us
    all_to_all x1, waiting for transfers between devices, per_device(): lax.all_to_all(jnp.broadcast_to(right[None], (n_seq, *right.shape)), 'seq...  3.9 us
    pallas_call x1, Pallas kernels, pair(): pl.pallas_call(functools.partial(pair_kernel, sizes), in_specs=[in_vmem]...  2.8 us
    pallas_call x1, Pallas kernels, project(): pl.pallas_call(project_kernel, in_specs=[pl.BlockSpec(memory_space=pltpu....  2.3 us
  transfers between devices with their start and end apart: 7, of which 6 were waited for; matrix products, arithmetic and copies ran while one was open for 2% of the time, Pallas kernels for 0%

profile of v6, /device:TPU:2, one launch (start us, length us, event | category | flops | bytes accessed | tf_op | source)
XLA Modules:
  0.0 56.4 jit_solution(8028538048875958632)
XLA Ops:
  0.0 2.3 %project.1 = bf16[2,32,256]{2,1,0:T(8,128)(2,1)} custom-call(bf16[256,256]{1,0:T(8,128)(2,1)} %bitcast.21, f32[1,256]{1,0:T(1,128)} %bitcast.24, f32[1,256]{1,0:T(1,128)} %bitcast.25, bf16[32,256]{1,0:T(8,128)(2,1)} %bitcast.22, f32[1,32]{1,0:T(1,128)} %bitcast.26, bf16[32,256]{1,0:T(8,128)(2,1)} %bitcast.23, f32[1,32]{1,0:T(1,128)} %bitcast.27), custom_call_target="tpu_custom_call" | custom-call | tf_op jit(solution)/shard_map/project/pallas_call | solution.py:72
  2.3 1.9 %collective-permute-start = (bf16[2,32,256]{2,1,0:T(8,128)(2,1)}, bf16[2,32,256]{2,1,0:T(8,128)(2,1)S(1)}, u32[]{:S(2)}, u32[]{:S(2)}) collective-permute-start(bf16[2,32,256]{2,1,0:T(8,128)(2,1)} %project.1), channel_id=1, source_target_pairs={{0,4},{1,5},{2,6},{3,7},{4,0},{5,1},{6,2},{7,3},{8,12},{9,13},{10,... | collective-permute-start | bytes 98312 | tf_op jit(solution)/shard_map/ppermute | solution.py:206
  4.2 0.7 %fusion = (bf16[1,32,256]{2,1,0:T(8,128)(2,1)S(1)}, bf16[1,32,256]{2,1,0:T(8,128)(2,1)S(1)}) fusion(bf16[2,32,256]{2,1,0:T(8,128)(2,1)} %project.1), kind=kLoop, calls=%fused_computation.4 | loop fusion | bytes 65536 | tf_op jit(solution)/shard_map/slice | solution.py:208
  5.0 0.6 %collective-permute-done = bf16[2,32,256]{2,1,0:T(8,128)(2,1)S(1)} collective-permute-done((bf16[2,32,256]{2,1,0:T(8,128)(2,1)}, bf16[2,32,256]{2,1,0:T(8,128)(2,1)S(1)}, u32[]{:S(2)}, u32[]{:S(2)}) %collective-permute-start) | collective-permute-done | bytes 32800 | tf_op jit(solution)/shard_map/ppermute | solution.py:206
  5.6 6.9 %collective-permute-start.1 = (bf16[2,32,256]{2,1,0:T(8,128)(2,1)S(1)}, bf16[2,32,256]{2,1,0:T(8,128)(2,1)S(1)}, u32[]{:S(2)}, u32[]{:S(2)}) collective-permute-start(bf16[2,32,256]{2,1,0:T(8,128)(2,1)S(1)} %pad_maximum_fusion.1), channel_id=1, source_target_pairs={{0,160},{1,161},{2,162},{3,163},{4,256},{5,257},{6,258},{7,259},{8... | collective-permute-start | bytes 98312 | tf_op jit(solution)/shard_map/ppermute | solution.py:206
  12.6 2.8 %collective-permute-done.1 = bf16[2,32,256]{2,1,0:T(8,128)(2,1)S(1)} collective-permute-done((bf16[2,32,256]{2,1,0:T(8,128)(2,1)S(1)}, bf16[2,32,256]{2,1,0:T(8,128)(2,1)S(1)}, u32[]{:S(2)}, u32[]{:S(2)}) %collective-permute-start.1) | collective-permute-done | bytes 32800 | tf_op jit(solution)/shard_map/ppermute | solution.py:206
  15.4 0.7 %broadcast_in_dim.4 = bf16[8,2,32,256]{3,2,1,0:T(8,128)(2,1)} broadcast(bf16[2,32,256]{2,1,0:T(8,128)(2,1)S(1)} %collective-permute-done.1), dimensions={1,2,3} | broadcast | bytes 294912 | tf_op jit(solution)/shard_map/broadcast_in_dim | solution.py:212
  16.1 6.7 %all-to-all-start = ((bf16[8,2,32,256]{3,2,1,0:T(8,128)(2,1)}), bf16[8,2,32,256]{3,2,1,0:T(8,128)(2,1)S(1)}, u32[]{:S(2)}, u32[]{:S(2)}) async-start(bf16[8,2,32,256]{3,2,1,0:T(8,128)(2,1)} %broadcast_in_dim.4), calls=%async_computation | async-start | bytes 524288 | tf_op jit(solution)/shard_map/all_to_all | solution.py:212
  22.8 3.7 %collective-permute-start.2 = (bf16[2,32,256]{2,1,0:T(8,128)(2,1)S(1)}, bf16[2,32,256]{2,1,0:T(8,128)(2,1)S(1)}, u32[]{:S(2)}, u32[]{:S(2)}) collective-permute-start(bf16[2,32,256]{2,1,0:T(8,128)(2,1)S(1)} %pad_maximum_fusion.2), channel_id=1, source_target_pairs={{0,24},{1,8},{2,0},{3,16},{4,12},{5,28},{6,20},{7,4},{8,1},{9,17},... | collective-permute-start | bytes 98312 | tf_op jit(solution)/shard_map/ppermute | solution.py:206
  26.6 3.0 %collective-permute-done.2.own_ref = bf16[2,32,256]{2,1,0:T(8,128)(2,1)S(1)} collective-permute-done((bf16[2,32,256]{2,1,0:T(8,128)(2,1)S(1)}, bf16[2,32,256]{2,1,0:T(8,128)(2,1)S(1)}, u32[]{:S(2)}, u32[]{:S(2)}) %collective-permute-start.2) | collective-permute-done | bytes 32800 | tf_op jit(solution)/shard_map/ppermute | solution.py:206
  29.6 0.0 all-to-all-done
  29.6 1.1 %broadcast_in_dim.5 = bf16[4,16,32,256]{3,2,1,0:T(8,128)(2,1)} broadcast(bf16[16,32,256]{2,1,0:T(8,128)(2,1)S(1)} %bitcast.18), dimensions={1,2,3} | broadcast | bytes 1310720 | tf_op jit(solution)/shard_map/broadcast_in_dim | solution.py:218
  30.7 0.0 copy-start.1
  30.7 9.7 %all-to-all-start.1 = ((bf16[4,16,32,256]{3,2,1,0:T(8,128)(2,1)}), bf16[4,16,32,256]{3,2,1,0:T(8,128)(2,1)S(1)}, u32[]{:S(2)}, u32[]{:S(2)}) async-start(bf16[4,16,32,256]{3,2,1,0:T(8,128)(2,1)} %broadcast_in_dim.5), calls=%async_computation.1 | async-start | bytes 2097152 | tf_op jit(solution)/shard_map/all_to_all | solution.py:218
  40.3 1.9 %collective-permute-start.3 = (bf16[2,32,256]{2,1,0:T(8,128)(2,1)S(1)}, bf16[2,32,256]{2,1,0:T(8,128)(2,1)S(1)}, u32[]{:S(2)}, u32[]{:S(2)}) collective-permute-start(bf16[2,32,256]{2,1,0:T(8,128)(2,1)S(1)} %collective-permute-done.2.own_ref), channel_id=1, source_target_pairs={{0,4},{1,5},{2,6},{3,7},{4,0},{5,1},{6,2},{7,3},{8,12},{9,13},{10,... | collective-permute-start | bytes 98312 | tf_op jit(solution)/shard_map/ppermute | solution.py:206
  42.2 1.2 %collective-permute-done.3.core_ref = bf16[2,32,256]{2,1,0:T(8,128)(2,1)S(1)} collective-permute-done((bf16[2,32,256]{2,1,0:T(8,128)(2,1)S(1)}, bf16[2,32,256]{2,1,0:T(8,128)(2,1)S(1)}, u32[]{:S(2)}, u32[]{:S(2)}) %collective-permute-start.3) | collective-permute-done | bytes 32800 | tf_op jit(solution)/shard_map/ppermute | solution.py:206
  43.4 3.2 %collective-permute-start.4 = (bf16[2,2,32,256]{3,2,1,0:T(8,128)(2,1)S(1)}, bf16[2,2,32,256]{3,2,1,0:T(8,128)(2,1)S(1)}, u32[]{:S(2)}, u32[]{:S(2)}) collective-permute-start(bf16[2,2,32,256]{3,2,1,0:T(8,128)(2,1)S(1)} %pad_maximum_fusion), channel_id=1, source_target_pairs={{0,8},{1,9},{2,10},{3,11},{4,12},{5,13},{6,14},{7,15},{8,0},{9,1},... | collective-permute-start | bytes 196616 | tf_op jit(solution)/shard_map/ppermute | solution.py:206
  46.6 0.0 copy-done.1
  46.6 0.1 copy.12
  46.7 0.1 copy.13.refs_2_
  46.9 2.7 %collective-permute-done.4.near_ref = bf16[2,2,32,256]{3,2,1,0:T(8,128)(2,1)S(1)} collective-permute-done((bf16[2,2,32,256]{3,2,1,0:T(8,128)(2,1)S(1)}, bf16[2,2,32,256]{3,2,1,0:T(8,128)(2,1)S(1)}, u32[]{:S(2)}, u32[]{:S(2)}) %collective-permute-start.4) | collective-permute-done | bytes 65568 | tf_op jit(solution)/shard_map/ppermute | solution.py:206
  49.6 0.1 turn.1.refs_0_
  49.7 0.0 copy-start
  49.7 3.9 %all-to-all-done.1.refs_1_ = bf16[4,16,32,256]{3,2,1,0:T(8,128)(2,1)S(1)} async-done(((bf16[4,16,32,256]{3,2,1,0:T(8,128)(2,1)}), bf16[4,16,32,256]{3,2,1,0:T(8,128)(2,1)S(1)}, u32[]{:S(2)}, u32[]{:S(2)}) %all-to-all-start.1) | async-done | bytes 1048608 | tf_op jit(solution)/shard_map/all_to_all | solution.py:218
  53.6 0.0 copy-done
  53.6 2.8 %pair.1 = bf16[16,128,128]{2,1,0:T(8,128)(2,1)} custom-call(bf16[512,128]{1,0:T(8,128)(2,1)S(1)} %turn.1.refs_0_, bf16[4,16,32,256]{3,2,1,0:T(8,128)(2,1)S(1)} %all-to-all-done.1.refs_1_, bf16[128,1024]{1,0:T(8,128)(2,1)S(1)} %copy.13.refs_2_, f32[1,128]{1,0:T(1,128)S(1)} %bitcast.17), custom_call_target="tpu_custom_call" | custom-call | tf_op jit(solution)/shard_map/pair/pallas_call | solution.py:160
  (5 shorter events, 0.1 us)
Async XLA Ops:
  2.3 3.3 %collective-permute-start = (bf16[2,32,256]{2,1,0:T(8,128)(2,1)}, bf16[2,32,256]{2,1,0:T(8,128)(2,1)S(1)}, u32[]{:S(2)}, u32[]{:S(2)}) collective-permute-start(bf16[2,32,256]{2,1,0:T(8,128)(2,1)} %project.1), channel_id=1, source_target_pairs={{0,4},{1,5},{2,6},{3,7},{4,0},{5,1},{6,2},{7,3},{8,12},{9,13},{10,... | collective-permute-start | bytes 98312 | tf_op jit(solution)/shard_map/ppermute | solution.py:206
  5.6 9.8 %collective-permute-start.1 = (bf16[2,32,256]{2,1,0:T(8,128)(2,1)S(1)}, bf16[2,32,256]{2,1,0:T(8,128)(2,1)S(1)}, u32[]{:S(2)}, u32[]{:S(2)}) collective-permute-start(bf16[2,32,256]{2,1,0:T(8,128)(2,1)S(1)} %pad_maximum_fusion.1), channel_id=1, source_target_pairs={{0,160},{1,161},{2,162},{3,163},{4,256},{5,257},{6,258},{7,259},{8... | collective-permute-start | bytes 98312 | tf_op jit(solution)/shard_map/ppermute | solution.py:206
  16.1 13.4 %all-to-all-start = ((bf16[8,2,32,256]{3,2,1,0:T(8,128)(2,1)}), bf16[8,2,32,256]{3,2,1,0:T(8,128)(2,1)S(1)}, u32[]{:S(2)}, u32[]{:S(2)}) async-start(bf16[8,2,32,256]{3,2,1,0:T(8,128)(2,1)} %broadcast_in_dim.4), calls=%async_computation | async-start | bytes 524288 | tf_op jit(solution)/shard_map/all_to_all | solution.py:212
  22.8 6.7 %collective-permute-start.2 = (bf16[2,32,256]{2,1,0:T(8,128)(2,1)S(1)}, bf16[2,32,256]{2,1,0:T(8,128)(2,1)S(1)}, u32[]{:S(2)}, u32[]{:S(2)}) collective-permute-start(bf16[2,32,256]{2,1,0:T(8,128)(2,1)S(1)} %pad_maximum_fusion.2), channel_id=1, source_target_pairs={{0,24},{1,8},{2,0},{3,16},{4,12},{5,28},{6,20},{7,4},{8,1},{9,17},... | collective-permute-start | bytes 98312 | tf_op jit(solution)/shard_map/ppermute | solution.py:206
  30.7 15.9 %copy-start.1 = (f32[1024,128]{1,0:T(8,128)S(1)}, f32[1024,128]{1,0:T(8,128)}, u32[]{:S(2)}) copy-start(f32[1024,128]{1,0:T(8,128)} %param.16) | copy-start | bytes 1572868
  30.7 22.9 %all-to-all-start.1 = ((bf16[4,16,32,256]{3,2,1,0:T(8,128)(2,1)}), bf16[4,16,32,256]{3,2,1,0:T(8,128)(2,1)S(1)}, u32[]{:S(2)}, u32[]{:S(2)}) async-start(bf16[4,16,32,256]{3,2,1,0:T(8,128)(2,1)} %broadcast_in_dim.5), calls=%async_computation.1 | async-start | bytes 2097152 | tf_op jit(solution)/shard_map/all_to_all | solution.py:218
  40.3 3.1 %collective-permute-start.3 = (bf16[2,32,256]{2,1,0:T(8,128)(2,1)S(1)}, bf16[2,32,256]{2,1,0:T(8,128)(2,1)S(1)}, u32[]{:S(2)}, u32[]{:S(2)}) collective-permute-start(bf16[2,32,256]{2,1,0:T(8,128)(2,1)S(1)} %collective-permute-done.2.own_ref), channel_id=1, source_target_pairs={{0,4},{1,5},{2,6},{3,7},{4,0},{5,1},{6,2},{7,3},{8,12},{9,13},{10,... | collective-permute-start | bytes 98312 | tf_op jit(solution)/shard_map/ppermute | solution.py:206
  43.4 6.2 %collective-permute-start.4 = (bf16[2,2,32,256]{3,2,1,0:T(8,128)(2,1)S(1)}, bf16[2,2,32,256]{3,2,1,0:T(8,128)(2,1)S(1)}, u32[]{:S(2)}, u32[]{:S(2)}) collective-permute-start(bf16[2,2,32,256]{3,2,1,0:T(8,128)(2,1)S(1)} %pad_maximum_fusion), channel_id=1, source_target_pairs={{0,8},{1,9},{2,10},{3,11},{4,12},{5,13},{6,14},{7,15},{8,0},{9,1},... | collective-permute-start | bytes 196616 | tf_op jit(solution)/shard_map/ppermute | solution.py:206
  49.7 3.9 %copy-start = (f32[128]{0:T(128)S(1)}, f32[128]{0:T(128)}, u32[]{:S(2)}) copy-start(f32[128]{0:T(128)} %param.17) | copy-start | bytes 1540
